TPU v7x, 32 devices: a whole 2x2x4 slice. The times are simulated.
32 devices in a mesh: parts: 2 (over y), aux: 4 (over x, core), occ: 4 (over z).
Axes of the slice: x: 2, y: 2, z: 4, core: 2. Of those that a mesh axis runs over, the one named last changes fastest.
Arguments:
- factors: bfloat16 [8, 896, 6144], P(('parts', 'aux'), 'occ'), parts along dimension 0, may hold values from -4 to 4
- block_mask: int32 [96, 8], P('parts'), parts along dimension 0, may hold values from 0 to 1, as said below
- block_lists: int32 [16, 24], P(('parts', 'occ')), parts along dimension 0, may hold values from -1 to 47, as said below
Outputs:
- exchange: float32 [12288, 6144], P(('parts', 'aux'), 'occ'), parts along dimension 0
There are 2 independent parts, one for each index of `parts`. A program takes and returns all parts, laid end to end along the dimension named above; each array names one. Nothing has to cross between parts.
Inputs may be any that keep to these rules, and one draw needn't show every extreme that they name: block_mask[b, o] is 1 exactly when b appears in block_lists[o]. `block_lists`: each row lists distinct kept basis blocks in increasing order, then -1 in its unused slots; some row fills all 24 slots.
All inputs are finite; a program needn't handle non-finite values.
Results may differ from a plain program's by a relative error of at most 0.0003.
Values may be sent and summed in bfloat16 or wider, within the bound.
No kernel may reach another device: no remote copies, remote signals or barrier semaphores. Data moves between devices by JAX's collectives and lax.ppermute only.
A program may use at most 192 MiB of HBM per device.

v0:
```python
import functools
import math

import jax
import jax.numpy as jnp
from jax import lax
from jax.experimental import pallas as pl
from jax.experimental.pallas import tpu as pltpu
from jax.sharding import PartitionSpec as P

BLK = 128
OBLK = 112
NB = 48
NOB = 8
PLACES = NOB * NB
STRIDE = 64
ROUNDS = 5
HOPS = ROUNDS - 1
LEVELS = (16, 18, 21, 48)
MIB = 1024 * 1024


def pick_kernel(lists, factors, *refs):
    items = refs[-1]
    orbitals, slots = lists.shape

    def step(slot, carry):
        for orbital in range(orbitals):
            block = jnp.maximum(lists[orbital, slot], 0)
            columns = pl.ds(pl.multiple_of(block * BLK, BLK), BLK)
            rows = slice(orbital * OBLK, (orbital + 1) * OBLK)
            items[orbital * slots + slot] = factors[0, rows, columns]
        return carry

    lax.fori_loop(0, slots, step, 0)


def pick(factors, block_lists, after=()):
    orbitals, slots = block_lists.shape
    count = orbitals * slots
    return pl.pallas_call(
        pick_kernel,
        grid_spec=pltpu.PrefetchScalarGridSpec(
            num_scalar_prefetch=1,
            grid=(),
            in_specs=[pl.BlockSpec(memory_space=pltpu.VMEM)]
            + [pl.BlockSpec(memory_space=pl.ANY)] * len(after),
            out_specs=pl.BlockSpec(memory_space=pltpu.VMEM),
        ),
        out_shape=jax.ShapeDtypeStruct((count, OBLK, BLK), factors.dtype),
        compiler_params=pltpu.CompilerParams(vmem_limit_bytes=16 * MIB),
        cost_estimate=pl.CostEstimate(
            flops=0, bytes_accessed=4 * count * OBLK * BLK, transcendentals=0
        ),
        name="pick",
    )(block_lists, factors, *after)


def as_number(condition):
    return jnp.where(condition, 1.0, 0.0)


def place_facts(shape, axis):
    place = lax.broadcasted_iota(jnp.int32, shape, axis).astype(jnp.float32)
    orbital = jnp.floor((place + 0.5) / NB)
    block = place - NB * orbital
    quarter = jnp.floor((block + 0.5) / (NB // 4))
    return place, orbital, quarter, jnp.floor((quarter + 0.5) / 2), jnp.floor((orbital + 0.5) / 2)


def plan_kernel(slots, where, masks, out):
    levels = 8
    rows = 2 * levels
    wide = (rows, PLACES)
    _, orbital, quarter, half, origin = place_facts(wide, 1)
    row = lax.broadcasted_iota(jnp.int32, wide, 0)
    kept = jnp.where(row < levels, masks[0:1, :], masks[1:2, :])
    capacity = jnp.zeros(wide, jnp.float32)
    for index, size in enumerate(LEVELS + LEVELS[-1:] * (levels - len(LEVELS))):
        capacity = jnp.where((row == index) | (row == index + levels), float(size), capacity)

    square = (PLACES, PLACES)
    down_place, down_orbital, _, _, _ = place_facts(square, 0)
    over_place, over_orbital, _, _, _ = place_facts(square, 1)
    same = as_number(down_orbital == over_orbital)
    before = as_number(down_place < over_place)
    within = (same * before).astype(jnp.bfloat16)
    same, before = same.astype(jnp.bfloat16), before.astype(jnp.bfloat16)

    def times(parts, matrix):
        stacked = jnp.concatenate(parts, axis=0).astype(jnp.bfloat16)
        product = jnp.dot(stacked, matrix, preferred_element_type=jnp.float32)
        return [product[index * rows:(index + 1) * rows] for index in range(len(parts))]

    touching = times([kept * as_number(quarter == z) for z in range(4)], same)
    need = [kept * as_number(touch > 0) for touch in touching]
    zero = jnp.zeros(wide, jnp.float32)

    def union(parts):
        best = zero
        for part in parts:
            best = jnp.maximum(best, part)
        return best

    x_need = []
    for x in range(2):
        touched = as_number(touching[2 * x] + touching[2 * x + 1] > 0)
        here = as_number(half == x)
        x_need.append([
            need[z] * jnp.maximum(here, as_number(quarter == z) * touched) for z in range(4)
        ])
    mine = [kept * as_number(origin == z) for z in range(4)]
    need_up = [union(need[z + 1:]) for z in range(4)]
    far_up = [union(need[z + 2:]) for z in range(4)]
    need_down = [union(need[:z]) for z in range(4)]
    far_down = [union(need[:max(z - 1, 0)]) for z in range(4)]
    up = [mine[z] * need_up[z] for z in range(4)]
    down = [mine[z] * need_down[z] for z in range(4)]
    cross = [[mine[z] * x_need[x][z] for z in range(4)] for x in range(2)]
    up_code, down_code = [zero] * 4, [zero] * 4
    cross_code = [[zero] * 4, [zero] * 4]

    for turn in range(ROUNDS):
        parts = []
        if turn < HOPS:
            for z in range(3):
                parts += [up[z] * far_up[z], up[z] - up[z] * far_up[z]]
                parts += [down[z + 1] * far_down[z + 1], down[z + 1] - down[z + 1] * far_down[z + 1]]
        parts += [cross[x][z] for x in range(2) for z in range(4)]
        ranks = iter(zip(parts, times(parts, before)))

        def taken(pairs):
            rank, total = zero, 0.0
            chosen = zero
            for part, counted in pairs:
                rank = rank + part * (counted + total)
                total = total + jnp.sum(part, axis=1, keepdims=True)
                chosen = chosen + part
            chosen = chosen * as_number(rank < capacity)
            return chosen, chosen * (rank + float(turn * STRIDE + 1))

        up_sent, down_sent = [], []
        if turn < HOPS:
            for z in range(3):
                sent, code = taken([next(ranks), next(ranks)])
                up_sent.append(sent)
                up_code[z] = up_code[z] + code
                up[z] = up[z] - sent
                sent, code = taken([next(ranks), next(ranks)])
                down_sent.append(sent)
                down_code[z + 1] = down_code[z + 1] + code
                down[z + 1] = down[z + 1] - sent
        for x in range(2):
            for z in range(4):
                sent, code = taken([next(ranks)])
                cross_code[x][z] = cross_code[x][z] + code
                cross[x][z] = cross[x][z] - sent
        if turn < HOPS:
            for z in range(3):
                up[z + 1] = up[z + 1] + up_sent[z] * need_up[z + 1]
                down[z] = down[z] + down_sent[z] * need_down[z]
                for x in range(2):
                    cross[x][z + 1] = cross[x][z + 1] + up_sent[z] * x_need[x][z + 1]
                    cross[x][z] = cross[x][z] + down_sent[z] * x_need[x][z]

    left = zero
    for part in up + down + cross[0] + cross[1]:
        left = left + part
    left = jnp.sum(left, axis=1, keepdims=True)
    left = left[:levels] + left[levels:]
    order = lax.broadcasted_iota(jnp.int32, (levels, 1), 0).astype(jnp.float32)
    level = jnp.min(jnp.where(left > 0, float(len(LEVELS) - 1), order), axis=0, keepdims=True)
    level_row = as_number(
        lax.broadcasted_iota(jnp.int32, (levels, PLACES), 0).astype(jnp.float32) == level
    )
    me_x, me_z = where[0] // 2, where[1]
    odd = lax.rem(me_z, 2).astype(jnp.float32)

    def at(parts, z):
        total = jnp.zeros((levels, PLACES), jnp.float32)
        for index, part in enumerate(parts):
            total = total + jnp.where(z == index, 1.0, 0.0) * part[:levels]
        return jnp.sum(total * level_row, axis=0, keepdims=True)

    cross_here = [jnp.where(me_x == 0, cross_code[0][z], cross_code[1][z]) for z in range(4)]
    cross_there = [jnp.where(me_x == 0, cross_code[1][z], cross_code[0][z]) for z in range(4)]
    def turn_of(code):
        return jnp.floor((code - 0.5) / STRIDE)

    got_up, got_down = at(up_code, me_z - 1), at(down_code, me_z + 1)
    got_cross = at(cross_here, me_z)
    inner = jnp.dot(kept.astype(jnp.bfloat16), within, preferred_element_type=jnp.float32)[0:1]
    one_orbital, one_origin = orbital[0:1], origin[0:1]
    slot = inner + slots * (one_orbital - 2 * one_origin)
    owned = kept[0:1] * as_number(one_origin == me_z.astype(jnp.float32))
    held = (
        owned * (slot + 1)
        + as_number(got_up > 0) * (got_up + STRIDE * (2 - odd + turn_of(got_up)))
        + as_number(got_down > 0) * (got_down + STRIDE * (1 + odd + turn_of(got_down)))
        - 1
    )
    crossed = got_cross - 1
    near = jnp.maximum(
        as_number(quarter[0:1] == where[0].astype(jnp.float32)),
        as_number(quarter[0:1] == me_z.astype(jnp.float32)),
    )
    arrival = jnp.maximum(
        as_number(got_up + got_down > 0) * turn_of(got_up + got_down),
        as_number(got_cross > 0) * turn_of(got_cross),
    )
    lane = lax.broadcasted_iota(jnp.int32, (1, PLACES), 1)
    stage = jnp.zeros((1, PLACES), jnp.float32)
    for index in range(NOB):
        inside = as_number(one_orbital == float(index)) * near * kept[0:1]
        stage = jnp.where(
            lane == index, jnp.max(arrival * inside, axis=1, keepdims=True), stage
        )

    buffer = jnp.floor((held + 0.5) / STRIDE)
    tall = (PLACES, PLACES)
    target = lax.broadcasted_iota(jnp.int32, tall, 0).astype(jnp.float32) + 1
    pair = jnp.concatenate([buffer, held - STRIDE * buffer] + [jnp.zeros_like(held)] * 6, axis=0)
    sends = []
    sent_up, sent_down = at(up_code, me_z), at(down_code, me_z)
    for sent in (
        jnp.where(odd > 0, sent_down, sent_up),
        jnp.where(odd > 0, sent_up, sent_down),
        at(cross_there, me_z),
    ):
        chosen = as_number(target == sent).astype(jnp.bfloat16)
        both = lax.dot_general(
            pair.astype(jnp.bfloat16), chosen, (((1,), (1,)), ((), ())),
            preferred_element_type=jnp.float32,
        )
        sends.append(both[0:1] * STRIDE + both[1:2])
    flat = level + jnp.zeros((1, PLACES), jnp.float32)
    result = jnp.concatenate(sends + [held, crossed, stage, flat, flat], axis=0)
    out[...] = result.astype(jnp.int32)


def plan(where, masks, slots):
    in_vmem = pl.BlockSpec(memory_space=pltpu.VMEM)
    return pl.pallas_call(
        functools.partial(plan_kernel, slots),
        grid_spec=pltpu.PrefetchScalarGridSpec(
            num_scalar_prefetch=1, grid=(), in_specs=[in_vmem], out_specs=in_vmem
        ),
        out_shape=jax.ShapeDtypeStruct((8, PLACES), jnp.int32),
        compiler_params=pltpu.CompilerParams(vmem_limit_bytes=16 * MIB),
        name="plan",
    )(where, masks)


def branch(which, low, high, run):
    if high - low == 1:
        run(low)
        return
    middle = (low + high) // 2

    @pl.when(which < middle)
    def _():
        branch(which, low, middle, run)

    @pl.when(which >= middle)
    def _():
        branch(which, middle, high, run)


def gather_kernel(turn, held, streams, passed, table, *refs):
    buffers, refs = refs[:held], refs[held:]
    arrived, outs = refs[:passed], refs[len(refs) - len(streams) - (passed > 0):]
    size = outs[0].shape[0]

    def step(index, carry):
        for stream, out in zip(streams, outs):
            code = table[stream * PLACES + turn * STRIDE + index]

            def run(n, out=out, code=code):
                out[index] = buffers[n][code & (STRIDE - 1)]

            branch(lax.shift_right_logical(code, 6), 0, held, run)
        for place in range(passed):
            outs[-1][place * size + index] = arrived[place][index]
        return carry

    lax.fori_loop(0, size, step, 0)


def gather(turn, size, table, buffers, streams, arrived, after):
    dtype = buffers[0].dtype
    shapes = [jax.ShapeDtypeStruct((size, OBLK, BLK), dtype) for _ in streams]
    if arrived:
        shapes.append(jax.ShapeDtypeStruct((size * len(arrived), OBLK, BLK), dtype))
    in_vmem = pl.BlockSpec(memory_space=pltpu.VMEM)
    return pl.pallas_call(
        functools.partial(gather_kernel, turn, len(buffers), streams, len(arrived)),
        grid_spec=pltpu.PrefetchScalarGridSpec(
            num_scalar_prefetch=1,
            grid=(),
            in_specs=[in_vmem] * (len(buffers) + len(arrived))
            + [pl.BlockSpec(memory_space=pl.ANY)] * len(after),
            out_specs=[in_vmem] * len(shapes),
        ),
        out_shape=shapes,
        compiler_params=pltpu.CompilerParams(
            vmem_limit_bytes=2 * sum(array.size for array in [*buffers, *arrived, *shapes]) + 4 * MIB
        ),
        cost_estimate=pl.CostEstimate(
            flops=0, bytes_accessed=4 * len(streams) * size * OBLK * BLK, transcendentals=0
        ),
        name="gather",
    )(table, *buffers, *arrived, *after)


def relay_kernel(source, token, out):
    out[...] = source[...]


def relay(source, token):
    in_vmem = pl.BlockSpec(memory_space=pltpu.VMEM)
    return pl.pallas_call(
        relay_kernel,
        in_specs=[in_vmem, pl.BlockSpec(memory_space=pl.ANY)],
        out_specs=in_vmem,
        out_shape=jax.ShapeDtypeStruct(source.shape, source.dtype),
        compiler_params=pltpu.CompilerParams(vmem_limit_bytes=16 * MIB),
        name="relay",
    )(source, token)


def product_kernel(
    groups, orbitals, row_blocks, col_blocks, stages, first, extra, loc, meta, *refs
):
    flat = iter(refs)
    before = None if first else next(flat)
    sources = [
        [[(next(flat), offset) for offset in offsets] for offsets in buffers] for buffers in groups
    ]
    for _ in range(extra):
        next(flat)
    out, done, items, acc, unit, state, in_sems, acc_sems, out_sems = flat
    group_aux = [len(buffers[0]) for buffers in groups]
    row_tile, col_tile = tile_of(row_blocks), tile_of(col_blocks)
    step_tile = unit.shape[0] // BLK
    col_tiles = col_blocks // col_tile
    first_row, first_col = meta[0], meta[1]
    room = items.shape[0]
    quad = math.gcd(row_blocks, col_blocks, 4)
    if quad == 1:
        quad = math.gcd(row_blocks, col_blocks)
    blocks, first_right = row_blocks + col_blocks, row_blocks
    if row_blocks == col_blocks:
        alike = first_row == first_col
        blocks = jnp.where(alike, row_blocks, blocks)
        first_right = jnp.where(alike, 0, first_right)
    depth = sum(group_aux) * OBLK
    padded = items.shape[2]
    height, width = row_tile * BLK, col_tile * BLK
    row_tiles = row_blocks // row_tile
    met_at, columns_at = orbitals, orbitals + row_tiles

    def code_of(group, orbital, block):
        return loc[group * PLACES + orbital * NB + block]

    def any_kept(orbital, start, count):
        best = code_of(0, orbital, start)
        for step in range(1, count):
            best = jnp.maximum(best, code_of(0, orbital, start + step))
        return best >= 0

    def whole_block(block):
        return jnp.where(block < row_blocks, first_row + block, first_col + block - row_blocks)

    def span_of(tile):
        return pl.ds(pl.multiple_of(tile * height, height), height)

    def entering(tile):
        return pltpu.make_async_copy(before.at[span_of(tile)], acc.at[span_of(tile)], acc_sems.at[tile])

    def leaving(tile):
        return pltpu.make_async_copy(acc.at[span_of(tile)], out.at[span_of(tile)], out_sems.at[tile])

    def survey(orbital, count):
        stage = loc[len(groups) * PLACES + orbital]
        wanted = jnp.logical_and(stage >= stages[0], stage <= stages[1])
        state[columns_at + count] = 0

        @pl.when(wanted)
        def _():
            @pl.when(any_kept(orbital, first_row, row_blocks))
            def _():
                columns = jnp.int32(0)
                for col in range(col_tiles):
                    held = any_kept(orbital, first_col + col * col_tile, col_tile)
                    columns = columns + jnp.where(held, 1 << col, 0)
                state[columns_at + count] = columns

        wanted = state[columns_at + count] > 0

        @pl.when(wanted)
        def _():
            state[count] = orbital
            for tile in range(row_tiles):
                held = any_kept(orbital, first_row + tile * row_tile, row_tile)
                state[met_at + tile] = state[met_at + tile] + jnp.where(held, 1 << count, 0)

        return count + jnp.where(wanted, 1, 0)

    for tile in range(row_tiles):
        state[met_at + tile] = 0
    count = lax.fori_loop(0, orbitals, survey, jnp.int32(0))
    done[...] = jnp.zeros(done.shape, done.dtype)

    def fetch(begin):
        def one(slot, carry):
            orbital = state[begin + slot]

            def load(block, run):
                start_aux = 0
                for group, buffers in enumerate(sources):
                    place = code_of(group, orbital, whole_block(block))

                    def copy(n, buffers=buffers, place=place, start_aux=start_aux):
                        for aux, (buffer, offset) in enumerate(buffers[n]):
                            pltpu.make_async_copy(
                                buffer.at[pl.ds((place & (STRIDE - 1)) + offset, run)],
                                items.at[
                                    slot, pl.ds(block, run), pl.ds((start_aux + aux) * OBLK, OBLK)
                                ],
                                in_sems.at[slot],
                            ).start()

                    branch(lax.shift_right_logical(place, 6), 0, len(buffers), copy)
                    start_aux += group_aux[group]
                if padded > depth:
                    items[slot, pl.ds(block, run), depth:] = jnp.zeros(
                        (run, padded - depth, BLK), items.dtype
                    )

            def step(part, carry):
                block = part * quad
                in_row = code_of(0, orbital, whole_block(block)) >= 0
                for group in range(len(groups)):
                    low = code_of(group, orbital, whole_block(block))
                    high = code_of(group, orbital, whole_block(block) + quad - 1)
                    in_row = jnp.logical_and(in_row, high - low == quad - 1)

                @pl.when(in_row)
                def _():
                    load(block, quad)

                @pl.when(jnp.logical_not(in_row))
                def _():
                    def single(inner, carry):
                        held = code_of(0, orbital, whole_block(block + inner)) >= 0

                        @pl.when(held)
                        def _():
                            load(block + inner, 1)

                        @pl.when(jnp.logical_not(held))
                        def _():
                            items[slot, block + inner] = jnp.zeros((padded, BLK), items.dtype)

                        return carry

                    lax.fori_loop(0, quad, single, 0)

                return carry

            return lax.fori_loop(0, blocks // quad, step, carry)

        lax.fori_loop(0, jnp.minimum(count - begin, room), one, 0)

    def landed(begin):
        def one(slot, carry):
            orbital = state[begin + slot]

            def step(block, carry):
                @pl.when(code_of(0, orbital, whole_block(block)) >= 0)
                def _():
                    whole = items.at[slot, block, pl.ds(0, depth)]
                    pltpu.make_async_copy(whole, whole, in_sems.at[slot]).wait()

                return carry

            return lax.fori_loop(0, blocks, step, carry)

        lax.fori_loop(0, jnp.minimum(count - begin, room), one, 0)

    def multiply(begin, tile):
        rows = span_of(tile)

        def one(slot, carry):
            @pl.when(lax.rem(lax.shift_right_logical(state[met_at + tile], begin + slot), 2) == 1)
            def _():
                turned = []
                for start in range(0, row_tile, step_tile):
                    left = jnp.concatenate(
                        [items[slot, tile * row_tile + start + step] for step in range(step_tile)],
                        axis=1,
                    )
                    turned.append(lax.dot_general(
                        unit[...], left, (((1,), (1,)), ((), ())), preferred_element_type=jnp.float32
                    ).astype(left.dtype))
                turned = jnp.concatenate(turned, axis=0)
                columns = state[columns_at + begin + slot]

                def column(col, carry):
                    @pl.when(lax.rem(lax.shift_right_logical(columns, col), 2) == 1)
                    def _():
                        right = jnp.concatenate(
                            [items[slot, first_right + col * col_tile + step] for step in range(col_tile)],
                            axis=1,
                        )
                        span = pl.ds(pl.multiple_of(col * width, width), width)
                        acc[rows, span] += jnp.dot(turned, right, preferred_element_type=jnp.float32)

                    return carry

                lax.fori_loop(0, col_tiles, column, 0)

            return carry

        lax.fori_loop(0, jnp.minimum(count - begin, room), one, 0)

    fetch(0)
    if first:
        def clear(tile, carry):
            acc[span_of(tile)] = jnp.zeros((height, acc.shape[1]), acc.dtype)
            return carry
    else:
        def clear(tile, carry):
            @pl.when(state[met_at + tile] > 0)
            def _():
                entering(tile).start()
            return carry

    lax.fori_loop(0, row_tiles, clear, 0)
    across = lax.broadcasted_iota(jnp.int32, unit.shape, 1)
    unit[...] = as_number(lax.broadcasted_iota(jnp.int32, unit.shape, 0) == across).astype(unit.dtype)
    passes = (count + room - 1) // room
    if first:
        passes = jnp.maximum(passes, 1)

    def one_pass(turn, carry):
        begin = turn * room

        @pl.when(turn > 0)
        def _():
            fetch(begin)

        landed(begin)

        def row_step(tile, carry):
            touched = jnp.logical_or(first, state[met_at + tile] > 0)

            @pl.when(touched)
            def _():
                if not first:
                    @pl.when(turn == 0)
                    def _():
                        entering(tile).wait()
                multiply(begin, tile)

                @pl.when(turn == passes - 1)
                def _():
                    leaving(tile).start()

            return carry

        lax.fori_loop(0, row_tiles, row_step, 0)
        return carry

    lax.fori_loop(0, passes, one_pass, 0)

    def row_end(tile, carry):
        @pl.when(jnp.logical_or(first, state[met_at + tile] > 0))
        def _():
            leaving(tile).wait()

        return carry

    lax.fori_loop(0, row_tiles, row_end, 0)


def tile_of(blocks):
    return 4 if blocks % 4 == 0 else 3 if blocks % 3 == 0 else 1


def product(loc, meta, sources, held, after, stages, orbitals, row_blocks, col_blocks):
    groups = [[[offset for _, offset in refs] for refs in group] for group in sources]
    flat = [array for group in sources for refs in group for array, _ in refs]
    total_aux = sum(len(group[0]) for group in sources)
    rows, cols = row_blocks * BLK, col_blocks * BLK
    row_tile = tile_of(row_blocks)
    step_tile = 2 if row_tile % 2 == 0 else row_tile
    row_tiles = row_blocks // row_tile
    padded = -(-total_aux * OBLK // 256) * 256
    room = 2
    first = held is None
    in_hbm = pl.BlockSpec(memory_space=pltpu.HBM)
    in_any = pl.BlockSpec(memory_space=pl.ANY)
    return pl.pallas_call(
        functools.partial(
            product_kernel, groups, orbitals, row_blocks, col_blocks, stages, first, len(after)
        ),
        grid_spec=pltpu.PrefetchScalarGridSpec(
            num_scalar_prefetch=2,
            grid=(),
            in_specs=[in_hbm] * (not first)
            + [in_any] * (len(flat) + len(after)),
            out_specs=[in_hbm, pl.BlockSpec(memory_space=pltpu.VMEM)],
            scratch_shapes=[
                pltpu.VMEM((room, row_blocks + col_blocks, padded, BLK), jnp.bfloat16),
                pltpu.VMEM((rows, cols), jnp.float32),
                pltpu.VMEM((step_tile * BLK, step_tile * BLK), jnp.bfloat16),
                pltpu.SMEM((2 * orbitals + row_tiles + 1,), jnp.int32),
                pltpu.SemaphoreType.DMA((room,)),
                pltpu.SemaphoreType.DMA((row_tiles,)),
                pltpu.SemaphoreType.DMA((row_tiles,)),
            ],
        ),
        out_shape=[
            jax.ShapeDtypeStruct((rows, cols), jnp.float32),
            jax.ShapeDtypeStruct((8, 128), jnp.float32),
        ],
        input_output_aliases={} if first else {2: 0},
        compiler_params=pltpu.CompilerParams(
            vmem_limit_bytes=2 * room * padded * (rows + cols) + 4 * rows * cols + 4 * MIB
        ),
        cost_estimate=pl.CostEstimate(
            flops=2 * rows * cols * total_aux * OBLK * orbitals,
            bytes_accessed=4 * rows * cols,
            transcendentals=0,
        ),
        name="product",
    )(loc, meta, *([] if first else [held]), *flat, *after)


def rounds(size, add, table, own):
    first = [(0, 1), (1, 0), (2, 3), (3, 2)]
    second = []
    for aux in range(4):
        here, there = aux * 4, (aux ^ 1) * 4
        second += [(here, there), (here + 1, here + 2), (here + 2, here + 1), (here + 3, there + 3)]
    across = [(0, 2), (2, 0), (1, 3), (3, 1)]

    def to_core(held):
        return lax.ppermute(held, "aux", first)

    moved, crossed, passed = [], [], []
    core_own = to_core(own)
    total, done = None, []
    calls = {2: (0, 1), 3: (2, 2), 4: (3, 3), 5: (4, 4)}
    if size == LEVELS[-1]:
        calls = {ROUNDS: (0, HOPS)}
    for turn in range(ROUNDS + 1):
        chunks = []
        if turn < ROUNDS:
            streams = (0, 1, 2) if turn < HOPS else (2,)
            arrived = moved[-2:] + crossed[-1:]
            chunks = gather(turn, size, table, [own] + moved, streams, arrived, done)
        if turn > 0:
            if turn < ROUNDS:
                passed.append(to_core(chunks[-1]))
            elif done:
                passed.append(to_core(relay(crossed[-1], done[0])))
            else:
                passed.append(to_core(crossed[-1]))
        if turn in calls:
            near = [[(own, 0), (core_own, 0)]]
            for index, held in enumerate(moved):
                near.append([(held, 0), (passed[index // 2], index % 2 * size)])
            far = [
                [(held, 0), (passed[index], 2 * size if index < HOPS else 0)]
                for index, held in enumerate(crossed)
            ]
            total, token = add(
                table[3 * PLACES:6 * PLACES], [near, far], total, chunks[:1], calls[turn]
            )
            done = [token]
        if turn < HOPS:
            moved.append(lax.ppermute(chunks[0], "occ", first))
            moved.append(lax.ppermute(chunks[1], ("aux", "occ"), second))
        if turn < ROUNDS:
            crossed.append(lax.ppermute(chunks[2 if turn < HOPS else 0], "aux", across))
    return total


def on_device(shape, factors, block_mask, block_lists):
    aux_count, occ_count = shape["aux"], shape["occ"]
    own_orbitals, slots = block_lists.shape
    aux, occ = lax.axis_index("aux"), lax.axis_index("occ")
    row_blocks, col_blocks = NB // aux_count, NB // occ_count
    meta = jnp.stack([aux * row_blocks, occ * col_blocks]).astype(jnp.int32)

    def add(loc, sources, held, after, stages):
        return product(loc, meta, sources, held, after, stages, NOB, row_blocks, col_blocks)

    kept = block_mask.T > 0
    if aux_count == 4 and occ_count == 4 and shape["parts"] == 2:
        mask = as_number(kept).reshape(1, PLACES)
        other = lax.ppermute(mask, "parts", [(0, 1), (1, 0)])
        where = jnp.stack([aux, occ]).astype(jnp.int32)
        table = plan(where, jnp.concatenate([mask, other]), slots)
        own = pick(factors, block_lists, [table])
        return lax.switch(
            table[6, 0],
            [functools.partial(rounds, size, add) for size in LEVELS],
            table.reshape(-1),
            own,
        )
    own = pick(factors, block_lists)
    everything = lax.all_gather(lax.all_gather(own, "aux"), "occ")
    sources = [[(everything[z, a], 0) for a in range(aux_count)] for z in range(occ_count)]
    earlier = jnp.arange(NB)[None, :] < jnp.arange(NB)[:, None]
    rank = jnp.sum(kept[:, None, :] & earlier[None], axis=2, dtype=jnp.int32)
    orbital = jnp.arange(NOB, dtype=jnp.int32)[:, None]
    start = orbital // own_orbitals * STRIDE + orbital % own_orbitals * slots
    loc = jnp.concatenate([
        jnp.where(kept, rank + start, -1).reshape(-1), jnp.zeros(PLACES, jnp.int32)
    ])
    return add(loc, [sources], None, [], (0, 0))[0]


def solution(mesh):
    placed = (P(("parts", "aux"), "occ", None), P("parts", None), P(("parts", "occ"), None))
    return jax.shard_map(
        functools.partial(on_device, dict(mesh.shape)),
        mesh=mesh,
        in_specs=placed,
        out_specs=P(("parts", "aux"), "occ"),
        check_vma=False,
    )
```

profile of v0, /device:TPU:8, one launch (start us, length us, event | category | flops | bytes accessed | tf_op | source)
XLA Modules:
  0.0 137.4 jit_solution(12840042307918219566)
XLA Ops:
  0.8 1.6 %collective-permute-start.76 = (f32[1,384]{1,0:T(1,128)S(1)}, f32[1,384]{1,0:T(1,128)S(1)}, u32[]{:S(2)}, u32[]{:S(2)}) collective-permute-start(f32[1,384]{1,0:T(1,128)S(1)} %reshape.9), channel_id=1, source_target_pairs={{0,16},{16,0},{1,17},{17,1},{2,18},{18,2},{3,19},{19,3},{4,20},{20... | collective-permute-start | bytes 4616 | tf_op jit(solution)/shard_map/ppermute | solution.py:704
  2.5 1.9 %collective-permute-done.76 = f32[1,384]{1,0:T(1,128)S(1)} collective-permute-done((f32[1,384]{1,0:T(1,128)S(1)}, f32[1,384]{1,0:T(1,128)S(1)}, u32[]{:S(2)}, u32[]{:S(2)}) %collective-permute-start.76) | collective-permute-done | bytes 1568 | tf_op jit(solution)/shard_map/ppermute | solution.py:704
  4.4 2.8 %plan.1.refs_0_ = s32[8,384]{1,0:T(8,128)S(1)} custom-call(s32[2]{0:T(128)S(1)} %pad_add_fusion.where, f32[2,384]{1,0:T(2,128)S(1)} %pad_maximum_fusion.masks), custom_call_target="tpu_custom_call" | custom-call | tf_op jit(solution)/shard_map/plan/pallas_call | solution.py:243
  7.8 1.8 %copy-done.20 = bf16[1,224,6144]{2,1,0:T(8,128)(2,1)S(1)} copy-done((bf16[1,224,6144]{2,1,0:T(8,128)(2,1)S(1)}, bf16[1,224,6144]{2,1,0:T(8,128)(2,1)}, u32[]{:S(2)}) %copy-start.20) | copy-done | bytes 2752536
  10.2 2.2 %pick.1 = bf16[48,112,128]{2,1,0:T(8,128)(2,1)} custom-call(s32[2,24]{1,0:T(2,128)S(1)} %copy-done.26, bf16[1,224,6144]{2,1,0:T(8,128)(2,1)S(1)} %copy-done.20, s32[8,384]{1,0:T(8,128)S(1)} %plan.1.refs_0_), custom_call_target="tpu_custom_call" | custom-call | bytes 2752512 | tf_op jit(solution)/shard_map/pick/pallas_call | solution.py:41
  13.0 124.2 %conditional.1 = (f32[1536,1536]{1,0:T(8,128)}) conditional(s32[]{:T(128)} %bitcast.3, (s32[8,384]{1,0:T(8,128)S(1)}, bf16[48,112,128]{2,1,0:T(8,128)(2,1)}, s32[2]{0:T(128)S(1)}) %tuple.17, (s32[8,384]{1,0:T(8,128)S(1)}, bf16[48,112,128]{2,1,0:T(8,128)(2,1)}, s32[2]{0:T(128)S(1)}) %tuple.17, ...), branch_computations={%region_0.1_spmd, %region_1.2_spmd, %region_2.3_spmd, %region_3.4_... | conditional | flops 67645734912 | bytes 315010400 | solution.py:708
  13.3 2.3 %gather.25 = (bf16[18,112,128]{2,1,0:T(8,128)(2,1)S(1)}, bf16[18,112,128]{2,1,0:T(8,128)(2,1)S(1)}, bf16[18,112,128]{2,1,0:T(8,128)(2,1)S(1)}) custom-call(s32[3072]{0:T(1024)S(1)} %reshape.12.table, bf16[48,112,128]{2,1,0:T(8,128)(2,1)} %get-tuple-element.63.refs_0_.refs_1_), custom_call_target="tpu_custom_call" | custom-call | bytes 3096576 | tf_op jit(solution)/shard_map/cond/branch_1_fun/gather/pallas_call | solution.py:295
  15.6 3.1 %collective-permute-start.21 = (bf16[18,112,128]{2,1,0:T(8,128)(2,1)S(1)}, bf16[18,112,128]{2,1,0:T(8,128)(2,1)S(1)}, u32[]{:S(2)}, u32[]{:S(2)}) collective-permute-start(bf16[18,112,128]{2,1,0:T(8,128)(2,1)S(1)} %get-tuple-element.65), channel_id=1, source_target_pairs={{0,4},{1,2},{2,1},{3,7},{4,0},{5,6},{6,5},{7,3},{8,12},{9,10},{10,... | collective-permute-start | bytes 1548296 | tf_op jit(solution)/shard_map/cond/branch_1_fun/ppermute | solution.py:685
  20.2 7.7 %collective-permute-done.20.refs_1_.refs_3_.refs_2_ = bf16[18,112,128]{2,1,0:T(8,128)(2,1)S(1)} collective-permute-done((bf16[18,112,128]{2,1,0:T(8,128)(2,1)S(1)}, bf16[18,112,128]{2,1,0:T(8,128)(2,1)S(1)}, u32[]{:S(2)}, u32[]{:S(2)}) %collective-permute-start.20) | collective-permute-done | bytes 516128 | tf_op jit(solution)/shard_map/cond/branch_1_fun/ppermute | solution.py:684
  30.5 4.4 %gather.26 = (bf16[18,112,128]{2,1,0:T(8,128)(2,1)S(1)}, bf16[18,112,128]{2,1,0:T(8,128)(2,1)S(1)}, bf16[18,112,128]{2,1,0:T(8,128)(2,1)S(1)}, bf16[54,112,128]{2,1,0:T(8,128)(2,1)}) custom-call(s32[3072]{0:T(1024)S(1)} %reshape.12.table, bf16[48,112,128]{2,1,0:T(8,128)(2,1)} %get-tuple-element.63.refs_0_.refs_1_, ...), custom_call_target="tpu_custom_call" | custom-call | bytes 3096576 | tf_op jit(solution)/shard_map/cond/branch_1_fun/gather/pallas_call | solution.py:295
  39.0 8.6 %collective-permute-done.24.refs_3_.refs_5_.refs_6_.refs_7_ = bf16[18,112,128]{2,1,0:T(8,128)(2,1)S(1)} collective-permute-done((bf16[18,112,128]{2,1,0:T(8,128)(2,1)S(1)}, bf16[18,112,128]{2,1,0:T(8,128)(2,1)S(1)}, u32[]{:S(2)}, u32[]{:S(2)}) %collective-permute-start.24) | collective-permute-done | bytes 516128 | tf_op jit(solution)/shard_map/cond/branch_1_fun/ppermute | solution.py:684
  50.3 4.8 %gather.27 = (bf16[18,112,128]{2,1,0:T(8,128)(2,1)S(1)}, bf16[18,112,128]{2,1,0:T(8,128)(2,1)S(1)}, bf16[18,112,128]{2,1,0:T(8,128)(2,1)S(1)}, bf16[54,112,128]{2,1,0:T(8,128)(2,1)}) custom-call(s32[3072]{0:T(1024)S(1)} %reshape.12.table, bf16[48,112,128]{2,1,0:T(8,128)(2,1)} %get-tuple-element.63.refs_0_.refs_1_, ...), custom_call_target="tpu_custom_call" | custom-call | bytes 3096576 | tf_op jit(solution)/shard_map/cond/branch_1_fun/gather/pallas_call | solution.py:295
  60.0 3.3 %collective-permute-done.19.refs_1_.refs_2_ = bf16[48,112,128]{2,1,0:T(8,128)(2,1)} collective-permute-done((bf16[48,112,128]{2,1,0:T(8,128)(2,1)}, bf16[48,112,128]{2,1,0:T(8,128)(2,1)}, u32[]{:S(2)}, u32[]{:S(2)}) %collective-permute-start.19) | collective-permute-done | bytes 1376288 | tf_op jit(solution)/shard_map/cond/branch_1_fun/ppermute | solution.py:650
  65.6 5.6 %product.17 = (f32[1536,1536]{1,0:T(8,128)}, f32[8,128]{1,0:T(8,128)S(1)}) custom-call(s32[1152]{0:T(1024)S(1)} %reshape.16.loc, s32[2]{0:T(128)S(1)} %get-tuple-element.62.meta, bf16[48,112,128]{2,1,0:T(8,128)(2,1)} %get-tuple-element.63.refs_0_.refs_1_, bf16[48,112,128]{2,1,0:T(8,128)(2,1)} %collective-permute-done.19.refs_1_.refs_2_, ...), custom_call_target="tpu_custom_call" | custom-call | flops 16911433728 | bytes 9437184 | tf_op jit(solution)/shard_map/cond/branch_1_fun/product/pallas_call | solution.py:604
  72.1 5.2 %collective-permute-done.28.refs_5_.refs_7_.refs_11_ = bf16[18,112,128]{2,1,0:T(8,128)(2,1)S(1)} collective-permute-done((bf16[18,112,128]{2,1,0:T(8,128)(2,1)}, bf16[18,112,128]{2,1,0:T(8,128)(2,1)S(1)}, u32[]{:S(2)}, u32[]{:S(2)}) %collective-permute-start.28) | collective-permute-done | bytes 516128 | tf_op jit(solution)/shard_map/cond/branch_1_fun/ppermute | solution.py:684
  77.2 3.5 %gather.28 = (bf16[18,112,128]{2,1,0:T(8,128)(2,1)S(1)}, bf16[18,112,128]{2,1,0:T(8,128)(2,1)S(1)}, bf16[18,112,128]{2,1,0:T(8,128)(2,1)S(1)}, bf16[54,112,128]{2,1,0:T(8,128)(2,1)S(1)}) custom-call(s32[3072]{0:T(1024)S(1)} %reshape.12.table, bf16[48,112,128]{2,1,0:T(8,128)(2,1)} %get-tuple-element.63.refs_0_.refs_1_, ...), custom_call_target="tpu_custom_call" | custom-call | bytes 3096576 | tf_op jit(solution)/shard_map/cond/branch_1_fun/gather/pallas_call | solution.py:295
  80.8 4.7 %collective-permute-start.31 = (bf16[54,112,128]{2,1,0:T(8,128)(2,1)S(1)}, bf16[54,112,128]{2,1,0:T(8,128)(2,1)S(1)}, u32[]{:S(2)}, u32[]{:S(2)}) collective-permute-start(bf16[54,112,128]{2,1,0:T(8,128)(2,1)S(1)} %get-tuple-element.77), channel_id=1, source_target_pairs={{0,4},{4,0},{8,12},{12,8},{1,5},{5,1},{9,13},{13,9},{2,6},{6,2},{1... | collective-permute-start | bytes 4644872 | tf_op jit(solution)/shard_map/cond/branch_1_fun/ppermute | solution.py:650
  85.4 3.9 %collective-permute-start.34 = (bf16[18,112,128]{2,1,0:T(8,128)(2,1)S(1)}, bf16[18,112,128]{2,1,0:T(8,128)(2,1)S(1)}, u32[]{:S(2)}, u32[]{:S(2)}) collective-permute-start(bf16[18,112,128]{2,1,0:T(8,128)(2,1)S(1)} %get-tuple-element.81), channel_id=1, source_target_pairs={{0,8},{8,0},{4,12},{12,4},{1,9},{9,1},{5,13},{13,5},{2,10},{10,2},... | collective-permute-start | bytes 1548296 | tf_op jit(solution)/shard_map/cond/branch_1_fun/ppermute | solution.py:687
  89.3 11.7 %product.18 = (f32[1536,1536]{1,0:T(8,128)}, f32[8,128]{1,0:T(8,128)S(1)}) custom-call(s32[1152]{0:T(1024)S(1)} %reshape.16.loc, s32[2]{0:T(128)S(1)} %get-tuple-element.62.meta, f32[1536,1536]{1,0:T(8,128)} %get-tuple-element.73.refs_0_, bf16[48,112,128]{2,1,0:T(8,128)(2,1)} %get-tuple-element.63.refs_0_.refs_1_, ...), custom_call_target="tpu_custom_call", output_to_operand_aliasing={{0}: (2, {})} | custom-call | flops 16911433728 | bytes 9437184 | tf_op jit(solution)/shard_map/cond/branch_1_fun/product/pallas_call | solution.py:604
  102.8 2.7 %gather.29 = (bf16[18,112,128]{2,1,0:T(8,128)(2,1)S(1)}, bf16[54,112,128]{2,1,0:T(8,128)(2,1)S(1)}) custom-call(s32[3072]{0:T(1024)S(1)} %reshape.12.table, bf16[48,112,128]{2,1,0:T(8,128)(2,1)} %get-tuple-element.63.refs_0_.refs_1_, bf16[18,112,128]{2,1,0:T(8,128)(2,1)S(1)} %collective-permute-done.20.refs_1_.refs_3_.refs_2_, ...), custom_call_target="tpu_custom_call" | custom-call | bytes 1032192 | tf_op jit(solution)/shard_map/cond/branch_1_fun/gather/pallas_call | solution.py:295
  105.9 3.0 %collective-permute-done.35.refs_16_.refs_18_.refs_26_ = bf16[54,112,128]{2,1,0:T(8,128)(2,1)S(1)} collective-permute-done((bf16[54,112,128]{2,1,0:T(8,128)(2,1)S(1)}, bf16[54,112,128]{2,1,0:T(8,128)(2,1)S(1)}, u32[]{:S(2)}, u32[]{:S(2)}) %collective-permute-start.35) | collective-permute-done | bytes 1548320 | tf_op jit(solution)/shard_map/cond/branch_1_fun/ppermute | solution.py:650
  110.2 9.6 %collective-permute-done.36.source.refs_27_ = bf16[18,112,128]{2,1,0:T(8,128)(2,1)S(1)} collective-permute-done((bf16[18,112,128]{2,1,0:T(8,128)(2,1)S(1)}, bf16[18,112,128]{2,1,0:T(8,128)(2,1)S(1)}, u32[]{:S(2)}, u32[]{:S(2)}) %collective-permute-start.36) | collective-permute-done | bytes 516128 | tf_op jit(solution)/shard_map/cond/branch_1_fun/ppermute | solution.py:687
  119.8 4.5 %collective-permute-start.37 = (bf16[18,112,128]{2,1,0:T(8,128)(2,1)S(1)}, bf16[18,112,128]{2,1,0:T(8,128)(2,1)S(1)}, u32[]{:S(2)}, u32[]{:S(2)}) collective-permute-start(bf16[18,112,128]{2,1,0:T(8,128)(2,1)S(1)} %relay.4), channel_id=1, source_target_pairs={{0,4},{4,0},{8,12},{12,8},{1,5},{5,1},{9,13},{13,9},{2,6},{6,2},{1... | collective-permute-start | bytes 1548296 | tf_op jit(solution)/shard_map/cond/branch_1_fun/ppermute | solution.py:650
  125.8 11.2 %product.20 = (f32[1536,1536]{1,0:T(8,128)}, f32[8,128]{1,0:T(8,128)}) custom-call(s32[1152]{0:T(1024)S(1)} %reshape.16.loc, s32[2]{0:T(128)S(1)} %get-tuple-element.62.meta, f32[1536,1536]{1,0:T(8,128)} %get-tuple-element.85.refs_0_, bf16[48,112,128]{2,1,0:T(8,128)(2,1)} %get-tuple-element.63.refs_0_.refs_1_, ...), custom_call_target="tpu_custom_call", output_to_operand_aliasing={{0}: (2, {})} | custom-call | flops 16911433728 | bytes 9437184 | tf_op jit(solution)/shard_map/cond/branch_1_fun/product/pallas_call | solution.py:604
  (50 shorter events, 26.2 us)
Async XLA Ops:
  0.8 3.6 %collective-permute-start.76 = (f32[1,384]{1,0:T(1,128)S(1)}, f32[1,384]{1,0:T(1,128)S(1)}, u32[]{:S(2)}, u32[]{:S(2)}) collective-permute-start(f32[1,384]{1,0:T(1,128)S(1)} %reshape.9), channel_id=1, source_target_pairs={{0,16},{16,0},{1,17},{17,1},{2,18},{18,2},{3,19},{19,3},{4,20},{20... | collective-permute-start | bytes 4616 | tf_op jit(solution)/shard_map/ppermute | solution.py:704
  7.8 1.8 %copy-start.20 = (bf16[1,224,6144]{2,1,0:T(8,128)(2,1)S(1)}, bf16[1,224,6144]{2,1,0:T(8,128)(2,1)}, u32[]{:S(2)}) copy-start(bf16[1,224,6144]{2,1,0:T(8,128)(2,1)} %factors.1) | copy-start | bytes 8257540
  15.5 12.4 %collective-permute-start.20 = (bf16[18,112,128]{2,1,0:T(8,128)(2,1)S(1)}, bf16[18,112,128]{2,1,0:T(8,128)(2,1)S(1)}, u32[]{:S(2)}, u32[]{:S(2)}) collective-permute-start(bf16[18,112,128]{2,1,0:T(8,128)(2,1)S(1)} %get-tuple-element.64), channel_id=1, source_target_pairs={{0,1},{1,0},{2,3},{3,2},{4,5},{5,4},{6,7},{7,6},{8,9},{9,8},{10,11... | collective-permute-start | bytes 1548296 | tf_op jit(solution)/shard_map/cond/branch_1_fun/ppermute | solution.py:684
  15.6 13.5 %collective-permute-start.21 = (bf16[18,112,128]{2,1,0:T(8,128)(2,1)S(1)}, bf16[18,112,128]{2,1,0:T(8,128)(2,1)S(1)}, u32[]{:S(2)}, u32[]{:S(2)}) collective-permute-start(bf16[18,112,128]{2,1,0:T(8,128)(2,1)S(1)} %get-tuple-element.65), channel_id=1, source_target_pairs={{0,4},{1,2},{2,1},{3,7},{4,0},{5,6},{6,5},{7,3},{8,12},{9,10},{10,... | collective-permute-start | bytes 1548296 | tf_op jit(solution)/shard_map/cond/branch_1_fun/ppermute | solution.py:685
  18.8 11.8 %collective-permute-start.22 = (bf16[18,112,128]{2,1,0:T(8,128)(2,1)S(1)}, bf16[18,112,128]{2,1,0:T(8,128)(2,1)S(1)}, u32[]{:S(2)}, u32[]{:S(2)}) collective-permute-start(bf16[18,112,128]{2,1,0:T(8,128)(2,1)S(1)} %get-tuple-element.66), channel_id=1, source_target_pairs={{0,8},{8,0},{4,12},{12,4},{1,9},{9,1},{5,13},{13,5},{2,10},{10,2},... | collective-permute-start | bytes 1548296 | tf_op jit(solution)/shard_map/cond/branch_1_fun/ppermute | solution.py:687
  34.9 12.7 %collective-permute-start.24 = (bf16[18,112,128]{2,1,0:T(8,128)(2,1)S(1)}, bf16[18,112,128]{2,1,0:T(8,128)(2,1)S(1)}, u32[]{:S(2)}, u32[]{:S(2)}) collective-permute-start(bf16[18,112,128]{2,1,0:T(8,128)(2,1)S(1)} %get-tuple-element.68), channel_id=1, source_target_pairs={{0,1},{1,0},{2,3},{3,2},{4,5},{5,4},{6,7},{7,6},{8,9},{9,8},{10,11... | collective-permute-start | bytes 1548296 | tf_op jit(solution)/shard_map/cond/branch_1_fun/ppermute | solution.py:684
  35.9 13.1 %collective-permute-start.25 = (bf16[18,112,128]{2,1,0:T(8,128)(2,1)S(1)}, bf16[18,112,128]{2,1,0:T(8,128)(2,1)S(1)}, u32[]{:S(2)}, u32[]{:S(2)}) collective-permute-start(bf16[18,112,128]{2,1,0:T(8,128)(2,1)S(1)} %get-tuple-element.69), channel_id=1, source_target_pairs={{0,4},{1,2},{2,1},{3,7},{4,0},{5,6},{6,5},{7,3},{8,12},{9,10},{10,... | collective-permute-start | bytes 1548296 | tf_op jit(solution)/shard_map/cond/branch_1_fun/ppermute | solution.py:685
  37.5 12.8 %collective-permute-start.26 = (bf16[18,112,128]{2,1,0:T(8,128)(2,1)S(1)}, bf16[18,112,128]{2,1,0:T(8,128)(2,1)S(1)}, u32[]{:S(2)}, u32[]{:S(2)}) collective-permute-start(bf16[18,112,128]{2,1,0:T(8,128)(2,1)S(1)} %get-tuple-element.70), channel_id=1, source_target_pairs={{0,8},{8,0},{4,12},{12,4},{1,9},{9,1},{5,13},{13,5},{2,10},{10,2},... | collective-permute-start | bytes 1548296 | tf_op jit(solution)/shard_map/cond/branch_1_fun/ppermute | solution.py:687
  39.0 25.5 %collective-permute-start.23 = (bf16[54,112,128]{2,1,0:T(8,128)(2,1)}, bf16[54,112,128]{2,1,0:T(8,128)(2,1)}, u32[]{:S(2)}, u32[]{:S(2)}) collective-permute-start(bf16[54,112,128]{2,1,0:T(8,128)(2,1)} %get-tuple-element.67), channel_id=1, source_target_pairs={{0,4},{4,0},{8,12},{12,8},{1,5},{5,1},{9,13},{13,9},{2,6},{6,2},{1... | collective-permute-start | bytes 4644872 | tf_op jit(solution)/shard_map/cond/branch_1_fun/ppermute | solution.py:650
  55.1 0.8 copy-start.31
  55.9 0.8 copy-start.33
  57.6 7.0 %collective-permute-start.27 = (bf16[54,112,128]{2,1,0:T(8,128)(2,1)}, bf16[54,112,128]{2,1,0:T(8,128)(2,1)}, u32[]{:S(2)}, u32[]{:S(2)}) collective-permute-start(bf16[54,112,128]{2,1,0:T(8,128)(2,1)} %get-tuple-element.71), channel_id=1, source_target_pairs={{0,4},{4,0},{8,12},{12,8},{1,5},{5,1},{9,13},{13,9},{2,6},{6,2},{1... | collective-permute-start | bytes 4644872 | tf_op jit(solution)/shard_map/cond/branch_1_fun/ppermute | solution.py:650
  57.6 5.7 %collective-permute-start.19 = (bf16[48,112,128]{2,1,0:T(8,128)(2,1)}, bf16[48,112,128]{2,1,0:T(8,128)(2,1)}, u32[]{:S(2)}, u32[]{:S(2)}) collective-permute-start(bf16[48,112,128]{2,1,0:T(8,128)(2,1)} %get-tuple-element.63.refs_0_.refs_1_), channel_id=1, source_target_pairs={{0,4},{4,0},{8,12},{12,8},{1,5},{5,1},{9,13},{13,9},{2,6},{6,2},{1... | collective-permute-start | bytes 4128776 | tf_op jit(solution)/shard_map/cond/branch_1_fun/ppermute | solution.py:650
  58.1 13.9 %collective-permute-start.29 = (bf16[18,112,128]{2,1,0:T(8,128)(2,1)}, bf16[18,112,128]{2,1,0:T(8,128)(2,1)S(1)}, u32[]{:S(2)}, u32[]{:S(2)}) collective-permute-start(bf16[18,112,128]{2,1,0:T(8,128)(2,1)} %copy-done.34), channel_id=1, source_target_pairs={{0,4},{1,2},{2,1},{3,7},{4,0},{5,6},{6,5},{7,3},{8,12},{9,10},{10,... | collective-permute-start | bytes 1548296 | tf_op jit(solution)/shard_map/cond/branch_1_fun/ppermute | solution.py:685
  58.4 13.7 %collective-permute-start.30 = (bf16[18,112,128]{2,1,0:T(8,128)(2,1)}, bf16[18,112,128]{2,1,0:T(8,128)(2,1)S(1)}, u32[]{:S(2)}, u32[]{:S(2)}) collective-permute-start(bf16[18,112,128]{2,1,0:T(8,128)(2,1)} %copy-done.33), channel_id=1, source_target_pairs={{0,8},{8,0},{4,12},{12,4},{1,9},{9,1},{5,13},{13,5},{2,10},{10,2},... | collective-permute-start | bytes 1548296 | tf_op jit(solution)/shard_map/cond/branch_1_fun/ppermute | solution.py:687
  63.2 14.0 %collective-permute-start.28 = (bf16[18,112,128]{2,1,0:T(8,128)(2,1)}, bf16[18,112,128]{2,1,0:T(8,128)(2,1)S(1)}, u32[]{:S(2)}, u32[]{:S(2)}) collective-permute-start(bf16[18,112,128]{2,1,0:T(8,128)(2,1)} %copy-done.31), channel_id=1, source_target_pairs={{0,1},{1,0},{2,3},{3,2},{4,5},{5,4},{6,7},{7,6},{8,9},{9,8},{10,11... | collective-permute-start | bytes 1548296 | tf_op jit(solution)/shard_map/cond/branch_1_fun/ppermute | solution.py:684
  64.5 1.1 copy-start.32
  80.8 8.5 %collective-permute-start.31 = (bf16[54,112,128]{2,1,0:T(8,128)(2,1)S(1)}, bf16[54,112,128]{2,1,0:T(8,128)(2,1)S(1)}, u32[]{:S(2)}, u32[]{:S(2)}) collective-permute-start(bf16[54,112,128]{2,1,0:T(8,128)(2,1)S(1)} %get-tuple-element.77), channel_id=1, source_target_pairs={{0,4},{4,0},{8,12},{12,8},{1,5},{5,1},{9,13},{13,9},{2,6},{6,2},{1... | collective-permute-start | bytes 4644872 | tf_op jit(solution)/shard_map/cond/branch_1_fun/ppermute | solution.py:650
  85.4 15.6 %collective-permute-start.33 = (bf16[18,112,128]{2,1,0:T(8,128)(2,1)S(1)}, bf16[18,112,128]{2,1,0:T(8,128)(2,1)S(1)}, u32[]{:S(2)}, u32[]{:S(2)}) collective-permute-start(bf16[18,112,128]{2,1,0:T(8,128)(2,1)S(1)} %get-tuple-element.80), channel_id=1, source_target_pairs={{0,4},{1,2},{2,1},{3,7},{4,0},{5,6},{6,5},{7,3},{8,12},{9,10},{10,... | collective-permute-start | bytes 1548296 | tf_op jit(solution)/shard_map/cond/branch_1_fun/ppermute | solution.py:685
  85.4 15.9 %collective-permute-start.34 = (bf16[18,112,128]{2,1,0:T(8,128)(2,1)S(1)}, bf16[18,112,128]{2,1,0:T(8,128)(2,1)S(1)}, u32[]{:S(2)}, u32[]{:S(2)}) collective-permute-start(bf16[18,112,128]{2,1,0:T(8,128)(2,1)S(1)} %get-tuple-element.81), channel_id=1, source_target_pairs={{0,8},{8,0},{4,12},{12,4},{1,9},{9,1},{5,13},{13,5},{2,10},{10,2},... | collective-permute-start | bytes 1548296 | tf_op jit(solution)/shard_map/cond/branch_1_fun/ppermute | solution.py:687
  89.3 13.5 %collective-permute-start.32 = (bf16[18,112,128]{2,1,0:T(8,128)(2,1)S(1)}, bf16[18,112,128]{2,1,0:T(8,128)(2,1)S(1)}, u32[]{:S(2)}, u32[]{:S(2)}) collective-permute-start(bf16[18,112,128]{2,1,0:T(8,128)(2,1)S(1)} %get-tuple-element.78.refs_21_), channel_id=1, source_target_pairs={{0,1},{1,0},{2,3},{3,2},{4,5},{5,4},{6,7},{7,6},{8,9},{9,8},{10,11... | collective-permute-start | bytes 1548296 | tf_op jit(solution)/shard_map/cond/branch_1_fun/ppermute | solution.py:684
  105.5 3.4 %collective-permute-start.35 = (bf16[54,112,128]{2,1,0:T(8,128)(2,1)S(1)}, bf16[54,112,128]{2,1,0:T(8,128)(2,1)S(1)}, u32[]{:S(2)}, u32[]{:S(2)}) collective-permute-start(bf16[54,112,128]{2,1,0:T(8,128)(2,1)S(1)} %get-tuple-element.83), channel_id=1, source_target_pairs={{0,4},{4,0},{8,12},{12,8},{1,5},{5,1},{9,13},{13,9},{2,6},{6,2},{1... | collective-permute-start | bytes 4644872 | tf_op jit(solution)/shard_map/cond/branch_1_fun/ppermute | solution.py:650
  105.6 14.2 %collective-permute-start.36 = (bf16[18,112,128]{2,1,0:T(8,128)(2,1)S(1)}, bf16[18,112,128]{2,1,0:T(8,128)(2,1)S(1)}, u32[]{:S(2)}, u32[]{:S(2)}) collective-permute-start(bf16[18,112,128]{2,1,0:T(8,128)(2,1)S(1)} %get-tuple-element.84.refs_27_), channel_id=1, source_target_pairs={{0,8},{8,0},{4,12},{12,4},{1,9},{9,1},{5,13},{13,5},{2,10},{10,2},... | collective-permute-start | bytes 1548296 | tf_op jit(solution)/shard_map/cond/branch_1_fun/ppermute | solution.py:687
  119.8 6.0 %collective-permute-start.37 = (bf16[18,112,128]{2,1,0:T(8,128)(2,1)S(1)}, bf16[18,112,128]{2,1,0:T(8,128)(2,1)S(1)}, u32[]{:S(2)}, u32[]{:S(2)}) collective-permute-start(bf16[18,112,128]{2,1,0:T(8,128)(2,1)S(1)} %relay.4), channel_id=1, source_target_pairs={{0,4},{4,0},{8,12},{12,8},{1,5},{5,1},{9,13},{13,9},{2,6},{6,2},{1... | collective-permute-start | bytes 1548296 | tf_op jit(solution)/shard_map/cond/branch_1_fun/ppermute | solution.py:650
  (2 other events, 1.5 us)
where the time goes:
time: 137 us
  Pallas kernels  52.3 us (38%)
  waiting for transfers between devices  48.8 us (36%)
  starting transfers between devices  27.5 us (20%)
  local copies, waits for them, and re-layouts  6.58 us (5%)
    pallas_call x4, Pallas kernels, product(): pl.pallas_call(functools.partial(product_kernel, groups, orbitals, row_bl...  29.7 us
    ppermute x4, waiting for transfers between devices, rounds(): moved.append(lax.ppermute(chunks[0], 'occ', first))  22.9 us
    pallas_call x5, Pallas kernels, gather(): pl.pallas_call(functools.partial(gather_kernel, turn, len(buffers), strea...  17.6 us
    ppermute x5, waiting for transfers between devices, rounds(): crossed.append(lax.ppermute(chunks[2 if turn < HOPS else 0], 'aux', across))  12.8 us
    ppermute x6, starting transfers between devices, to_core(): return lax.ppermute(held, 'aux', first)  9.73 us
    ppermute x5, starting transfers between devices, rounds(): crossed.append(lax.ppermute(chunks[2 if turn < HOPS else 0], 'aux', across))  8.75 us
    ppermute x6, waiting for transfers between devices, to_core(): return lax.ppermute(held, 'aux', first)  7.81 us
    ppermute x4, starting transfers between devices, rounds(): moved.append(lax.ppermute(chunks[1], ('aux', 'occ'), second))  5.05 us
  transfers between devices with their start and end apart: 20, of which 16 were waited for; matrix products, arithmetic and copies ran while one was open for 0% of the time, Pallas kernels for 17%

commit v1 on v0

--- a/solution.py
+++ b/solution.py
@@ -16,7 +16,8 @@
 STRIDE = 64
 ROUNDS = 5
 HOPS = ROUNDS - 1
-LEVELS = (16, 18, 21, 48)
+LEVELS = (15, 18, 21, 48)
+RUN = 3
 MIB = 1024 * 1024
 
 
@@ -219,7 +220,10 @@
     buffer = jnp.floor((held + 0.5) / STRIDE)
     tall = (PLACES, PLACES)
     target = lax.broadcasted_iota(jnp.int32, tall, 0).astype(jnp.float32) + 1
-    pair = jnp.concatenate([buffer, held - STRIDE * buffer] + [jnp.zeros_like(held)] * 6, axis=0)
+    blank = jnp.zeros_like(held)
+    pair = jnp.concatenate([buffer, held - STRIDE * buffer, blank + 1] + [blank] * 5, axis=0)
+    position = lax.broadcasted_iota(jnp.int32, (1, PLACES), 1).astype(jnp.float32)
+    spare = position - STRIDE * jnp.floor((position + 0.5) / STRIDE)
     sends = []
     sent_up, sent_down = at(up_code, me_z), at(down_code, me_z)
     for sent in (
@@ -232,7 +236,8 @@
             pair.astype(jnp.bfloat16), chosen, (((1,), (1,)), ((), ())),
             preferred_element_type=jnp.float32,
         )
-        sends.append(both[0:1] * STRIDE + both[1:2])
+        filled = both[0:1] * STRIDE + both[1:2]
+        sends.append(jnp.where(both[2:3] > 0, filled, spare))
     flat = level + jnp.zeros((1, PLACES), jnp.float32)
     result = jnp.concatenate(sends + [held, crossed, stage, flat, flat], axis=0)
     out[...] = result.astype(jnp.int32)
@@ -268,22 +273,49 @@
 
 def gather_kernel(turn, held, streams, passed, table, *refs):
     buffers, refs = refs[:held], refs[held:]
-    arrived, outs = refs[:passed], refs[len(refs) - len(streams) - (passed > 0):]
+    arrived, sems = refs[:passed], refs[-1]
+    outs = refs[len(refs) - 1 - len(streams) - (passed > 0):-1]
     size = outs[0].shape[0]
-
-    def step(index, carry):
-        for stream, out in zip(streams, outs):
-            code = table[stream * PLACES + turn * STRIDE + index]
-
-            def run(n, out=out, code=code):
-                out[index] = buffers[n][code & (STRIDE - 1)]
-
-            branch(lax.shift_right_logical(code, 6), 0, held, run)
-        for place in range(passed):
-            outs[-1][place * size + index] = arrived[place][index]
+    for place in range(passed):
+        span = pl.ds(place * size, size)
+        pltpu.make_async_copy(arrived[place], outs[-1].at[span], sems.at[len(outs) - 1]).start()
+
+    def load(stream, at, code, run):
+        def copy(n):
+            pltpu.make_async_copy(
+                buffers[n].at[pl.ds(code & (STRIDE - 1), run)],
+                outs[stream].at[pl.ds(at, run)],
+                sems.at[stream],
+            ).start()
+
+        branch(lax.shift_right_logical(code, 6), 0, held, copy)
+
+    def step(part, carry):
+        at = part * RUN
+        for index, stream in enumerate(streams):
+            start = stream * PLACES + turn * STRIDE + at
+            codes = [table[start + inner] for inner in range(RUN)]
+            in_row = codes[1] - codes[0] == 1
+            for inner in range(2, RUN):
+                in_row = jnp.logical_and(in_row, codes[inner] - codes[inner - 1] == 1)
+
+            @pl.when(in_row)
+            def _(index=index, codes=codes):
+                load(index, at, codes[0], RUN)
+
+            @pl.when(jnp.logical_not(in_row))
+            def _(index=index, start=start):
+                def single(inner, carry):
+                    load(index, at + inner, table[start + inner], 1)
+                    return carry
+
+                lax.fori_loop(0, RUN, single, 0)
+
         return carry
 
-    lax.fori_loop(0, size, step, 0)
+    lax.fori_loop(0, size // RUN, step, 0)
+    for index, out in enumerate(outs):
+        pltpu.make_async_copy(out, out, sems.at[index]).wait()
 
 
 def gather(turn, size, table, buffers, streams, arrived, after):
@@ -291,19 +323,18 @@
     shapes = [jax.ShapeDtypeStruct((size, OBLK, BLK), dtype) for _ in streams]
     if arrived:
         shapes.append(jax.ShapeDtypeStruct((size * len(arrived), OBLK, BLK), dtype))
-    in_vmem = pl.BlockSpec(memory_space=pltpu.VMEM)
     return pl.pallas_call(
         functools.partial(gather_kernel, turn, len(buffers), streams, len(arrived)),
         grid_spec=pltpu.PrefetchScalarGridSpec(
             num_scalar_prefetch=1,
             grid=(),
-            in_specs=[in_vmem] * (len(buffers) + len(arrived))
-            + [pl.BlockSpec(memory_space=pl.ANY)] * len(after),
-            out_specs=[in_vmem] * len(shapes),
+            in_specs=[pl.BlockSpec(memory_space=pl.ANY)] * (len(buffers) + len(arrived) + len(after)),
+            out_specs=[pl.BlockSpec(memory_space=pltpu.VMEM)] * len(shapes),
+            scratch_shapes=[pltpu.SemaphoreType.DMA((len(shapes),))],
         ),
         out_shape=shapes,
         compiler_params=pltpu.CompilerParams(
-            vmem_limit_bytes=2 * sum(array.size for array in [*buffers, *arrived, *shapes]) + 4 * MIB
+            vmem_limit_bytes=2 * sum(array.size for array in shapes) + 2 * MIB
         ),
         cost_estimate=pl.CostEstimate(
             flops=0, bytes_accessed=4 * len(streams) * size * OBLK * BLK, transcendentals=0
@@ -704,7 +735,7 @@
         other = lax.ppermute(mask, "parts", [(0, 1), (1, 0)])
         where = jnp.stack([aux, occ]).astype(jnp.int32)
         table = plan(where, jnp.concatenate([mask, other]), slots)
-        own = pick(factors, block_lists, [table])
+        own = pick(factors, block_lists)
         return lax.switch(
             table[6, 0],
             [functools.partial(rounds, size, add) for size in LEVELS],

time: 137 us -> 134 us (0.978); the launches traced: 137 us -> 133 us
  Pallas kernels: 52.3 us -> 43.5 us
  starting transfers between devices: 27.5 us -> 31.2 us
    pallas_call x4, Pallas kernels: 29.7 us -> 19.1 us  [product(): pl.pallas_call(functools.partial(product_kernel, groups, orbitals, row_bl...]
    ppermute x5, waiting for transfers between devices: 12.8 us -> 16.2 us  [rounds(): crossed.append(lax.ppermute(chunks[2 if turn < HOPS else 0], 'aux', across))]
    ppermute x5, starting transfers between devices: 8.75 us -> 12 us  [rounds(): crossed.append(lax.ppermute(chunks[2 if turn < HOPS else 0], 'aux', across))]
    ppermute x1, waiting for transfers between devices: 1.91 us -> 0.01 us  [on_device(): other = lax.ppermute(mask, 'parts', [(0, 1), (1, 0)])]
    pallas_call x5, Pallas kernels: 17.6 us -> 19.3 us  [gather(): pl.pallas_call(functools.partial(gather_kernel, turn, len(buffers), strea...]
    ppermute x4, waiting for transfers between devices: 3.39 us -> 1.75 us  [rounds(): moved.append(lax.ppermute(chunks[1], ('aux', 'occ'), second))]
  transfers between devices with their start and end apart: 20 -> 20, of which waited for: 16 -> 13; matrix products, arithmetic and copies ran while one was open for 0% -> 0% of each run, Pallas kernels for 17% -> 18%
where the time goes in v1:
time: 134 us; the launch traced here: 133 us
  waiting for transfers between devices  48.7 us (36%)
  Pallas kernels  43.5 us (32%)
  starting transfers between devices  31.2 us (23%)
  local copies, waits for them, and re-layouts  6.59 us (5%)
    ppermute x4, waiting for transfers between devices, rounds(): moved.append(lax.ppermute(chunks[0], 'occ', first))  22.9 us
    pallas_call x5, Pallas kernels, gather(): pl.pallas_call(functools.partial(gather_kernel, turn, len(buffers), strea...  19.3 us
    pallas_call x4, Pallas kernels, product(): pl.pallas_call(functools.partial(product_kernel, groups, orbitals, row_bl...  19.1 us
    ppermute x5, waiting for transfers between devices, rounds(): crossed.append(lax.ppermute(chunks[2 if turn < HOPS else 0], 'aux', across))  16.2 us
    ppermute x5, starting transfers between devices, rounds(): crossed.append(lax.ppermute(chunks[2 if turn < HOPS else 0], 'aux', across))  12 us
    ppermute x6, starting transfers between devices, to_core(): return lax.ppermute(held, 'aux', first)  8.67 us
    ppermute x6, waiting for transfers between devices, to_core(): return lax.ppermute(held, 'aux', first)  7.91 us
    ppermute x4, starting transfers between devices, rounds(): moved.append(lax.ppermute(chunks[1], ('aux', 'occ'), second))  5.51 us
  transfers between devices with their start and end apart: 20, of which 13 were waited for; matrix products, arithmetic and copies ran while one was open for 0% of the time, Pallas kernels for 18%

profile of v1, /device:TPU:8, one launch (start us, length us, event | category | flops | bytes accessed | tf_op | source)
XLA Modules:
  0.0 132.6 jit_solution(15152318609670603436)
XLA Ops:
  2.5 1.8 %copy-done.20 = bf16[1,224,6144]{2,1,0:T(8,128)(2,1)S(1)} copy-done((bf16[1,224,6144]{2,1,0:T(8,128)(2,1)S(1)}, bf16[1,224,6144]{2,1,0:T(8,128)(2,1)}, u32[]{:S(2)}) %copy-start.20) | copy-done | bytes 2752536
  5.0 2.2 %pick.1 = bf16[48,112,128]{2,1,0:T(8,128)(2,1)} custom-call(s32[2,24]{1,0:T(2,128)S(1)} %copy-done.26, bf16[1,224,6144]{2,1,0:T(8,128)(2,1)S(1)} %copy-done.20), custom_call_target="tpu_custom_call" | custom-call | bytes 2752512 | tf_op jit(solution)/shard_map/pick/pallas_call | solution.py:42
  7.1 2.8 %plan.1 = s32[8,384]{1,0:T(8,128)S(1)} custom-call(s32[2]{0:T(128)S(1)} %pad_add_fusion.where, f32[2,384]{1,0:T(2,128)S(1)} %pad_maximum_fusion.masks), custom_call_target="tpu_custom_call" | custom-call | tf_op jit(solution)/shard_map/plan/pallas_call | solution.py:248
  11.1 121.3 %conditional.1 = (f32[1536,1536]{1,0:T(8,128)}) conditional(s32[]{:T(128)} %bitcast.3, (s32[8,384]{1,0:T(8,128)S(1)}, bf16[48,112,128]{2,1,0:T(8,128)(2,1)}, s32[2]{0:T(128)S(1)}) %tuple.17, (s32[8,384]{1,0:T(8,128)S(1)}, bf16[48,112,128]{2,1,0:T(8,128)(2,1)}, s32[2]{0:T(128)S(1)}) %tuple.17, ...), branch_computations={%region_0.1_spmd, %region_1.2_spmd, %region_2.3_spmd, %region_3.4_... | conditional | flops 67645734912 | bytes 315010400 | solution.py:739
  11.3 2.3 %gather.25 = (bf16[18,112,128]{2,1,0:T(8,128)(2,1)S(1)}, bf16[18,112,128]{2,1,0:T(8,128)(2,1)S(1)}, bf16[18,112,128]{2,1,0:T(8,128)(2,1)S(1)}) custom-call(s32[3072]{0:T(1024)S(1)} %reshape.12.table, bf16[48,112,128]{2,1,0:T(8,128)(2,1)} %get-tuple-element.63.refs_0_.refs_1_), custom_call_target="tpu_custom_call" | custom-call | bytes 3096576 | tf_op jit(solution)/shard_map/cond/branch_1_fun/gather/pallas_call | solution.py:326
  14.1 2.7 %collective-permute-start.21 = (bf16[18,112,128]{2,1,0:T(8,128)(2,1)S(1)}, bf16[18,112,128]{2,1,0:T(8,128)(2,1)S(1)}, u32[]{:S(2)}, u32[]{:S(2)}) collective-permute-start(bf16[18,112,128]{2,1,0:T(8,128)(2,1)S(1)} %get-tuple-element.65), channel_id=1, source_target_pairs={{0,4},{1,2},{2,1},{3,7},{4,0},{5,6},{6,5},{7,3},{8,12},{9,10},{10,... | collective-permute-start | bytes 1548296 | tf_op jit(solution)/shard_map/cond/branch_1_fun/ppermute | solution.py:716
  18.3 8.6 %collective-permute-done.20.refs_1_.refs_3_.refs_2_ = bf16[18,112,128]{2,1,0:T(8,128)(2,1)S(1)} collective-permute-done((bf16[18,112,128]{2,1,0:T(8,128)(2,1)S(1)}, bf16[18,112,128]{2,1,0:T(8,128)(2,1)S(1)}, u32[]{:S(2)}, u32[]{:S(2)}) %collective-permute-start.20) | collective-permute-done | bytes 516128 | tf_op jit(solution)/shard_map/cond/branch_1_fun/ppermute | solution.py:715
  29.5 5.9 %gather.26 = (bf16[18,112,128]{2,1,0:T(8,128)(2,1)S(1)}, bf16[18,112,128]{2,1,0:T(8,128)(2,1)S(1)}, bf16[18,112,128]{2,1,0:T(8,128)(2,1)S(1)}, bf16[54,112,128]{2,1,0:T(8,128)(2,1)}) custom-call(s32[3072]{0:T(1024)S(1)} %reshape.12.table, bf16[48,112,128]{2,1,0:T(8,128)(2,1)} %get-tuple-element.63.refs_0_.refs_1_, ...), custom_call_target="tpu_custom_call" | custom-call | bytes 3096576 | tf_op jit(solution)/shard_map/cond/branch_1_fun/gather/pallas_call | solution.py:326
  37.5 9.6 %collective-permute-done.24.refs_3_.refs_5_.refs_6_.refs_7_ = bf16[18,112,128]{2,1,0:T(8,128)(2,1)S(1)} collective-permute-done((bf16[18,112,128]{2,1,0:T(8,128)(2,1)S(1)}, bf16[18,112,128]{2,1,0:T(8,128)(2,1)S(1)}, u32[]{:S(2)}, u32[]{:S(2)}) %collective-permute-start.24) | collective-permute-done | bytes 516128 | tf_op jit(solution)/shard_map/cond/branch_1_fun/ppermute | solution.py:715
  49.2 4.9 %gather.27 = (bf16[18,112,128]{2,1,0:T(8,128)(2,1)S(1)}, bf16[18,112,128]{2,1,0:T(8,128)(2,1)S(1)}, bf16[18,112,128]{2,1,0:T(8,128)(2,1)S(1)}, bf16[54,112,128]{2,1,0:T(8,128)(2,1)}) custom-call(s32[3072]{0:T(1024)S(1)} %reshape.12.table, bf16[48,112,128]{2,1,0:T(8,128)(2,1)} %get-tuple-element.63.refs_0_.refs_1_, ...), custom_call_target="tpu_custom_call" | custom-call | bytes 3096576 | tf_op jit(solution)/shard_map/cond/branch_1_fun/gather/pallas_call | solution.py:326
  59.3 3.0 %collective-permute-done.19.refs_1_.refs_2_ = bf16[48,112,128]{2,1,0:T(8,128)(2,1)} collective-permute-done((bf16[48,112,128]{2,1,0:T(8,128)(2,1)}, bf16[48,112,128]{2,1,0:T(8,128)(2,1)}, u32[]{:S(2)}, u32[]{:S(2)}) %collective-permute-start.19) | collective-permute-done | bytes 1376288 | tf_op jit(solution)/shard_map/cond/branch_1_fun/ppermute | solution.py:681
  62.3 2.9 %collective-permute-start.28 = (bf16[18,112,128]{2,1,0:T(8,128)(2,1)}, bf16[18,112,128]{2,1,0:T(8,128)(2,1)S(1)}, u32[]{:S(2)}, u32[]{:S(2)}) collective-permute-start(bf16[18,112,128]{2,1,0:T(8,128)(2,1)} %copy-done.31), channel_id=1, source_target_pairs={{0,1},{1,0},{2,3},{3,2},{4,5},{5,4},{6,7},{7,6},{8,9},{9,8},{10,11... | collective-permute-start | bytes 1548296 | tf_op jit(solution)/shard_map/cond/branch_1_fun/ppermute | solution.py:715
  66.3 7.9 %product.17 = (f32[1536,1536]{1,0:T(8,128)}, f32[8,128]{1,0:T(8,128)S(1)}) custom-call(s32[1152]{0:T(1024)S(1)} %reshape.16.loc, s32[2]{0:T(128)S(1)} %get-tuple-element.62.meta, bf16[48,112,128]{2,1,0:T(8,128)(2,1)} %get-tuple-element.63.refs_0_.refs_1_, bf16[48,112,128]{2,1,0:T(8,128)(2,1)} %collective-permute-done.19.refs_1_.refs_2_, ...), custom_call_target="tpu_custom_call" | custom-call | flops 16911433728 | bytes 9437184 | tf_op jit(solution)/shard_map/cond/branch_1_fun/product/pallas_call | solution.py:635
  74.3 3.2 %collective-permute-done.28.refs_5_.refs_7_.refs_11_ = bf16[18,112,128]{2,1,0:T(8,128)(2,1)S(1)} collective-permute-done((bf16[18,112,128]{2,1,0:T(8,128)(2,1)}, bf16[18,112,128]{2,1,0:T(8,128)(2,1)S(1)}, u32[]{:S(2)}, u32[]{:S(2)}) %collective-permute-start.28) | collective-permute-done | bytes 516128 | tf_op jit(solution)/shard_map/cond/branch_1_fun/ppermute | solution.py:715
  77.5 3.3 %gather.28 = (bf16[18,112,128]{2,1,0:T(8,128)(2,1)S(1)}, bf16[18,112,128]{2,1,0:T(8,128)(2,1)S(1)}, bf16[18,112,128]{2,1,0:T(8,128)(2,1)S(1)}, bf16[54,112,128]{2,1,0:T(8,128)(2,1)S(1)}) custom-call(s32[3072]{0:T(1024)S(1)} %reshape.12.table, bf16[48,112,128]{2,1,0:T(8,128)(2,1)} %get-tuple-element.63.refs_0_.refs_1_, ...), custom_call_target="tpu_custom_call" | custom-call | bytes 3096576 | tf_op jit(solution)/shard_map/cond/branch_1_fun/gather/pallas_call | solution.py:326
  81.8 8.1 %collective-permute-start.34 = (bf16[18,112,128]{2,1,0:T(8,128)(2,1)S(1)}, bf16[18,112,128]{2,1,0:T(8,128)(2,1)S(1)}, u32[]{:S(2)}, u32[]{:S(2)}) collective-permute-start(bf16[18,112,128]{2,1,0:T(8,128)(2,1)S(1)} %get-tuple-element.81), channel_id=1, source_target_pairs={{0,8},{8,0},{4,12},{12,4},{1,9},{9,1},{5,13},{13,5},{2,10},{10,2},... | collective-permute-start | bytes 1548296 | tf_op jit(solution)/shard_map/cond/branch_1_fun/ppermute | solution.py:718
  89.9 8.3 %product.18 = (f32[1536,1536]{1,0:T(8,128)}, f32[8,128]{1,0:T(8,128)S(1)}) custom-call(s32[1152]{0:T(1024)S(1)} %reshape.16.loc, s32[2]{0:T(128)S(1)} %get-tuple-element.62.meta, f32[1536,1536]{1,0:T(8,128)} %get-tuple-element.73.refs_0_, bf16[48,112,128]{2,1,0:T(8,128)(2,1)} %get-tuple-element.63.refs_0_.refs_1_, ...), custom_call_target="tpu_custom_call", output_to_operand_aliasing={{0}: (2, {})} | custom-call | flops 16911433728 | bytes 9437184 | tf_op jit(solution)/shard_map/cond/branch_1_fun/product/pallas_call | solution.py:635
  98.3 3.7 %collective-permute-done.34.refs_11_.refs_25_ = bf16[18,112,128]{2,1,0:T(8,128)(2,1)S(1)} collective-permute-done((bf16[18,112,128]{2,1,0:T(8,128)(2,1)S(1)}, bf16[18,112,128]{2,1,0:T(8,128)(2,1)S(1)}, u32[]{:S(2)}, u32[]{:S(2)}) %collective-permute-start.34) | collective-permute-done | bytes 516128 | tf_op jit(solution)/shard_map/cond/branch_1_fun/ppermute | solution.py:718
  103.5 2.9 %gather.29 = (bf16[18,112,128]{2,1,0:T(8,128)(2,1)S(1)}, bf16[54,112,128]{2,1,0:T(8,128)(2,1)S(1)}) custom-call(s32[3072]{0:T(1024)S(1)} %reshape.12.table, bf16[48,112,128]{2,1,0:T(8,128)(2,1)} %get-tuple-element.63.refs_0_.refs_1_, bf16[18,112,128]{2,1,0:T(8,128)(2,1)S(1)} %collective-permute-done.20.refs_1_.refs_3_.refs_2_, ...), custom_call_target="tpu_custom_call" | custom-call | bytes 1032192 | tf_op jit(solution)/shard_map/cond/branch_1_fun/gather/pallas_call | solution.py:326
  106.4 8.0 %collective-permute-start.35 = (bf16[54,112,128]{2,1,0:T(8,128)(2,1)S(1)}, bf16[54,112,128]{2,1,0:T(8,128)(2,1)S(1)}, u32[]{:S(2)}, u32[]{:S(2)}) collective-permute-start(bf16[54,112,128]{2,1,0:T(8,128)(2,1)S(1)} %get-tuple-element.83), channel_id=1, source_target_pairs={{0,4},{4,0},{8,12},{12,8},{1,5},{5,1},{9,13},{13,9},{2,6},{6,2},{1... | collective-permute-start | bytes 4644872 | tf_op jit(solution)/shard_map/cond/branch_1_fun/ppermute | solution.py:681
  114.4 3.0 %collective-permute-done.35.refs_16_.refs_18_.refs_26_ = bf16[54,112,128]{2,1,0:T(8,128)(2,1)S(1)} collective-permute-done((bf16[54,112,128]{2,1,0:T(8,128)(2,1)S(1)}, bf16[54,112,128]{2,1,0:T(8,128)(2,1)S(1)}, u32[]{:S(2)}, u32[]{:S(2)}) %collective-permute-start.35) | collective-permute-done | bytes 1548320 | tf_op jit(solution)/shard_map/cond/branch_1_fun/ppermute | solution.py:681
  118.6 9.6 %collective-permute-done.36.source.refs_27_ = bf16[18,112,128]{2,1,0:T(8,128)(2,1)S(1)} collective-permute-done((bf16[18,112,128]{2,1,0:T(8,128)(2,1)S(1)}, bf16[18,112,128]{2,1,0:T(8,128)(2,1)S(1)}, u32[]{:S(2)}, u32[]{:S(2)}) %collective-permute-start.36) | collective-permute-done | bytes 516128 | tf_op jit(solution)/shard_map/cond/branch_1_fun/ppermute | solution.py:718
  128.3 1.9 %collective-permute-done.37.refs_28_ = bf16[18,112,128]{2,1,0:T(8,128)(2,1)S(1)} collective-permute-done((bf16[18,112,128]{2,1,0:T(8,128)(2,1)S(1)}, bf16[18,112,128]{2,1,0:T(8,128)(2,1)S(1)}, u32[]{:S(2)}, u32[]{:S(2)}) %collective-permute-start.37) | collective-permute-done | bytes 516128 | tf_op jit(solution)/shard_map/cond/branch_1_fun/ppermute | solution.py:681
  130.2 1.7 %product.20 = (f32[1536,1536]{1,0:T(8,128)}, f32[8,128]{1,0:T(8,128)}) custom-call(s32[1152]{0:T(1024)S(1)} %reshape.16.loc, s32[2]{0:T(128)S(1)} %get-tuple-element.62.meta, f32[1536,1536]{1,0:T(8,128)} %get-tuple-element.85.refs_0_, bf16[48,112,128]{2,1,0:T(8,128)(2,1)} %get-tuple-element.63.refs_0_.refs_1_, ...), custom_call_target="tpu_custom_call", output_to_operand_aliasing={{0}: (2, {})} | custom-call | flops 16911433728 | bytes 9437184 | tf_op jit(solution)/shard_map/cond/branch_1_fun/product/pallas_call | solution.py:635
  (50 shorter events, 22.4 us)
Async XLA Ops:
  0.8 6.4 %collective-permute-start.76 = (f32[1,384]{1,0:T(1,128)S(1)}, f32[1,384]{1,0:T(1,128)S(1)}, u32[]{:S(2)}, u32[]{:S(2)}) collective-permute-start(f32[1,384]{1,0:T(1,128)S(1)} %reshape.9), channel_id=1, source_target_pairs={{0,16},{16,0},{1,17},{17,1},{2,18},{18,2},{3,19},{19,3},{4,20},{20... | collective-permute-start | bytes 4616 | tf_op jit(solution)/shard_map/ppermute | solution.py:735
  2.5 1.8 %copy-start.20 = (bf16[1,224,6144]{2,1,0:T(8,128)(2,1)S(1)}, bf16[1,224,6144]{2,1,0:T(8,128)(2,1)}, u32[]{:S(2)}) copy-start(bf16[1,224,6144]{2,1,0:T(8,128)(2,1)} %factors.1) | copy-start | bytes 8257540
  13.6 13.3 %collective-permute-start.20 = (bf16[18,112,128]{2,1,0:T(8,128)(2,1)S(1)}, bf16[18,112,128]{2,1,0:T(8,128)(2,1)S(1)}, u32[]{:S(2)}, u32[]{:S(2)}) collective-permute-start(bf16[18,112,128]{2,1,0:T(8,128)(2,1)S(1)} %get-tuple-element.64), channel_id=1, source_target_pairs={{0,1},{1,0},{2,3},{3,2},{4,5},{5,4},{6,7},{7,6},{8,9},{9,8},{10,11... | collective-permute-start | bytes 1548296 | tf_op jit(solution)/shard_map/cond/branch_1_fun/ppermute | solution.py:715
  14.1 13.9 %collective-permute-start.21 = (bf16[18,112,128]{2,1,0:T(8,128)(2,1)S(1)}, bf16[18,112,128]{2,1,0:T(8,128)(2,1)S(1)}, u32[]{:S(2)}, u32[]{:S(2)}) collective-permute-start(bf16[18,112,128]{2,1,0:T(8,128)(2,1)S(1)} %get-tuple-element.65), channel_id=1, source_target_pairs={{0,4},{1,2},{2,1},{3,7},{4,0},{5,6},{6,5},{7,3},{8,12},{9,10},{10,... | collective-permute-start | bytes 1548296 | tf_op jit(solution)/shard_map/cond/branch_1_fun/ppermute | solution.py:716
  16.8 12.6 %collective-permute-start.22 = (bf16[18,112,128]{2,1,0:T(8,128)(2,1)S(1)}, bf16[18,112,128]{2,1,0:T(8,128)(2,1)S(1)}, u32[]{:S(2)}, u32[]{:S(2)}) collective-permute-start(bf16[18,112,128]{2,1,0:T(8,128)(2,1)S(1)} %get-tuple-element.66), channel_id=1, source_target_pairs={{0,8},{8,0},{4,12},{12,4},{1,9},{9,1},{5,13},{13,5},{2,10},{10,2},... | collective-permute-start | bytes 1548296 | tf_op jit(solution)/shard_map/cond/branch_1_fun/ppermute | solution.py:718
  35.4 11.8 %collective-permute-start.24 = (bf16[18,112,128]{2,1,0:T(8,128)(2,1)S(1)}, bf16[18,112,128]{2,1,0:T(8,128)(2,1)S(1)}, u32[]{:S(2)}, u32[]{:S(2)}) collective-permute-start(bf16[18,112,128]{2,1,0:T(8,128)(2,1)S(1)} %get-tuple-element.68), channel_id=1, source_target_pairs={{0,1},{1,0},{2,3},{3,2},{4,5},{5,4},{6,7},{7,6},{8,9},{9,8},{10,11... | collective-permute-start | bytes 1548296 | tf_op jit(solution)/shard_map/cond/branch_1_fun/ppermute | solution.py:715
  35.5 12.3 %collective-permute-start.25 = (bf16[18,112,128]{2,1,0:T(8,128)(2,1)S(1)}, bf16[18,112,128]{2,1,0:T(8,128)(2,1)S(1)}, u32[]{:S(2)}, u32[]{:S(2)}) collective-permute-start(bf16[18,112,128]{2,1,0:T(8,128)(2,1)S(1)} %get-tuple-element.69), channel_id=1, source_target_pairs={{0,4},{1,2},{2,1},{3,7},{4,0},{5,6},{6,5},{7,3},{8,12},{9,10},{10,... | collective-permute-start | bytes 1548296 | tf_op jit(solution)/shard_map/cond/branch_1_fun/ppermute | solution.py:716
  36.4 12.8 %collective-permute-start.26 = (bf16[18,112,128]{2,1,0:T(8,128)(2,1)S(1)}, bf16[18,112,128]{2,1,0:T(8,128)(2,1)S(1)}, u32[]{:S(2)}, u32[]{:S(2)}) collective-permute-start(bf16[18,112,128]{2,1,0:T(8,128)(2,1)S(1)} %get-tuple-element.70), channel_id=1, source_target_pairs={{0,8},{8,0},{4,12},{12,4},{1,9},{9,1},{5,13},{13,5},{2,10},{10,2},... | collective-permute-start | bytes 1548296 | tf_op jit(solution)/shard_map/cond/branch_1_fun/ppermute | solution.py:718
  37.5 27.7 %collective-permute-start.23 = (bf16[54,112,128]{2,1,0:T(8,128)(2,1)}, bf16[54,112,128]{2,1,0:T(8,128)(2,1)}, u32[]{:S(2)}, u32[]{:S(2)}) collective-permute-start(bf16[54,112,128]{2,1,0:T(8,128)(2,1)} %get-tuple-element.67), channel_id=1, source_target_pairs={{0,4},{4,0},{8,12},{12,8},{1,5},{5,1},{9,13},{13,9},{2,6},{6,2},{1... | collective-permute-start | bytes 4644872 | tf_op jit(solution)/shard_map/cond/branch_1_fun/ppermute | solution.py:681
  54.2 0.8 copy-start.31
  55.0 0.8 copy-start.33
  56.6 8.6 %collective-permute-start.27 = (bf16[54,112,128]{2,1,0:T(8,128)(2,1)}, bf16[54,112,128]{2,1,0:T(8,128)(2,1)}, u32[]{:S(2)}, u32[]{:S(2)}) collective-permute-start(bf16[54,112,128]{2,1,0:T(8,128)(2,1)} %get-tuple-element.71), channel_id=1, source_target_pairs={{0,4},{4,0},{8,12},{12,8},{1,5},{5,1},{9,13},{13,9},{2,6},{6,2},{1... | collective-permute-start | bytes 4644872 | tf_op jit(solution)/shard_map/cond/branch_1_fun/ppermute | solution.py:681
  56.6 5.7 %collective-permute-start.19 = (bf16[48,112,128]{2,1,0:T(8,128)(2,1)}, bf16[48,112,128]{2,1,0:T(8,128)(2,1)}, u32[]{:S(2)}, u32[]{:S(2)}) collective-permute-start(bf16[48,112,128]{2,1,0:T(8,128)(2,1)} %get-tuple-element.63.refs_0_.refs_1_), channel_id=1, source_target_pairs={{0,4},{4,0},{8,12},{12,8},{1,5},{5,1},{9,13},{13,9},{2,6},{6,2},{1... | collective-permute-start | bytes 4128776 | tf_op jit(solution)/shard_map/cond/branch_1_fun/ppermute | solution.py:681
  57.2 17.1 %collective-permute-start.29 = (bf16[18,112,128]{2,1,0:T(8,128)(2,1)}, bf16[18,112,128]{2,1,0:T(8,128)(2,1)S(1)}, u32[]{:S(2)}, u32[]{:S(2)}) collective-permute-start(bf16[18,112,128]{2,1,0:T(8,128)(2,1)} %copy-done.34), channel_id=1, source_target_pairs={{0,4},{1,2},{2,1},{3,7},{4,0},{5,6},{6,5},{7,3},{8,12},{9,10},{10,... | collective-permute-start | bytes 1548296 | tf_op jit(solution)/shard_map/cond/branch_1_fun/ppermute | solution.py:716
  58.0 16.2 %collective-permute-start.30 = (bf16[18,112,128]{2,1,0:T(8,128)(2,1)}, bf16[18,112,128]{2,1,0:T(8,128)(2,1)S(1)}, u32[]{:S(2)}, u32[]{:S(2)}) collective-permute-start(bf16[18,112,128]{2,1,0:T(8,128)(2,1)} %copy-done.33), channel_id=1, source_target_pairs={{0,8},{8,0},{4,12},{12,4},{1,9},{9,1},{5,13},{13,5},{2,10},{10,2},... | collective-permute-start | bytes 1548296 | tf_op jit(solution)/shard_map/cond/branch_1_fun/ppermute | solution.py:718
  62.3 15.2 %collective-permute-start.28 = (bf16[18,112,128]{2,1,0:T(8,128)(2,1)}, bf16[18,112,128]{2,1,0:T(8,128)(2,1)S(1)}, u32[]{:S(2)}, u32[]{:S(2)}) collective-permute-start(bf16[18,112,128]{2,1,0:T(8,128)(2,1)} %copy-done.31), channel_id=1, source_target_pairs={{0,1},{1,0},{2,3},{3,2},{4,5},{5,4},{6,7},{7,6},{8,9},{9,8},{10,11... | collective-permute-start | bytes 1548296 | tf_op jit(solution)/shard_map/cond/branch_1_fun/ppermute | solution.py:715
  65.2 1.1 copy-start.32
  80.8 9.1 %collective-permute-start.31 = (bf16[54,112,128]{2,1,0:T(8,128)(2,1)S(1)}, bf16[54,112,128]{2,1,0:T(8,128)(2,1)S(1)}, u32[]{:S(2)}, u32[]{:S(2)}) collective-permute-start(bf16[54,112,128]{2,1,0:T(8,128)(2,1)S(1)} %get-tuple-element.77), channel_id=1, source_target_pairs={{0,4},{4,0},{8,12},{12,8},{1,5},{5,1},{9,13},{13,9},{2,6},{6,2},{1... | collective-permute-start | bytes 4644872 | tf_op jit(solution)/shard_map/cond/branch_1_fun/ppermute | solution.py:681
  80.9 17.4 %collective-permute-start.33 = (bf16[18,112,128]{2,1,0:T(8,128)(2,1)S(1)}, bf16[18,112,128]{2,1,0:T(8,128)(2,1)S(1)}, u32[]{:S(2)}, u32[]{:S(2)}) collective-permute-start(bf16[18,112,128]{2,1,0:T(8,128)(2,1)S(1)} %get-tuple-element.80), channel_id=1, source_target_pairs={{0,4},{1,2},{2,1},{3,7},{4,0},{5,6},{6,5},{7,3},{8,12},{9,10},{10,... | collective-permute-start | bytes 1548296 | tf_op jit(solution)/shard_map/cond/branch_1_fun/ppermute | solution.py:716
  81.8 20.2 %collective-permute-start.34 = (bf16[18,112,128]{2,1,0:T(8,128)(2,1)S(1)}, bf16[18,112,128]{2,1,0:T(8,128)(2,1)S(1)}, u32[]{:S(2)}, u32[]{:S(2)}) collective-permute-start(bf16[18,112,128]{2,1,0:T(8,128)(2,1)S(1)} %get-tuple-element.81), channel_id=1, source_target_pairs={{0,8},{8,0},{4,12},{12,4},{1,9},{9,1},{5,13},{13,5},{2,10},{10,2},... | collective-permute-start | bytes 1548296 | tf_op jit(solution)/shard_map/cond/branch_1_fun/ppermute | solution.py:718
  89.9 13.5 %collective-permute-start.32 = (bf16[18,112,128]{2,1,0:T(8,128)(2,1)S(1)}, bf16[18,112,128]{2,1,0:T(8,128)(2,1)S(1)}, u32[]{:S(2)}, u32[]{:S(2)}) collective-permute-start(bf16[18,112,128]{2,1,0:T(8,128)(2,1)S(1)} %get-tuple-element.78.refs_21_), channel_id=1, source_target_pairs={{0,1},{1,0},{2,3},{3,2},{4,5},{5,4},{6,7},{7,6},{8,9},{9,8},{10,11... | collective-permute-start | bytes 1548296 | tf_op jit(solution)/shard_map/cond/branch_1_fun/ppermute | solution.py:715
  106.4 11.0 %collective-permute-start.35 = (bf16[54,112,128]{2,1,0:T(8,128)(2,1)S(1)}, bf16[54,112,128]{2,1,0:T(8,128)(2,1)S(1)}, u32[]{:S(2)}, u32[]{:S(2)}) collective-permute-start(bf16[54,112,128]{2,1,0:T(8,128)(2,1)S(1)} %get-tuple-element.83), channel_id=1, source_target_pairs={{0,4},{4,0},{8,12},{12,8},{1,5},{5,1},{9,13},{13,9},{2,6},{6,2},{1... | collective-permute-start | bytes 4644872 | tf_op jit(solution)/shard_map/cond/branch_1_fun/ppermute | solution.py:681
  114.4 13.7 %collective-permute-start.36 = (bf16[18,112,128]{2,1,0:T(8,128)(2,1)S(1)}, bf16[18,112,128]{2,1,0:T(8,128)(2,1)S(1)}, u32[]{:S(2)}, u32[]{:S(2)}) collective-permute-start(bf16[18,112,128]{2,1,0:T(8,128)(2,1)S(1)} %get-tuple-element.84.refs_27_), channel_id=1, source_target_pairs={{0,8},{8,0},{4,12},{12,4},{1,9},{9,1},{5,13},{13,5},{2,10},{10,2},... | collective-permute-start | bytes 1548296 | tf_op jit(solution)/shard_map/cond/branch_1_fun/ppermute | solution.py:718
  128.2 2.0 %collective-permute-start.37 = (bf16[18,112,128]{2,1,0:T(8,128)(2,1)S(1)}, bf16[18,112,128]{2,1,0:T(8,128)(2,1)S(1)}, u32[]{:S(2)}, u32[]{:S(2)}) collective-permute-start(bf16[18,112,128]{2,1,0:T(8,128)(2,1)S(1)} %relay.4), channel_id=1, source_target_pairs={{0,4},{4,0},{8,12},{12,8},{1,5},{5,1},{9,13},{13,9},{2,6},{6,2},{1... | collective-permute-start | bytes 1548296 | tf_op jit(solution)/shard_map/cond/branch_1_fun/ppermute | solution.py:681
  (2 other events, 1.5 us)

commit v2 on v1

--- a/solution.py
+++ b/solution.py
@@ -70,15 +70,14 @@
 
 
 def plan_kernel(slots, where, masks, out):
-    levels = 8
-    rows = 2 * levels
+    rows = levels = 8
     wide = (rows, PLACES)
     _, orbital, quarter, half, origin = place_facts(wide, 1)
     row = lax.broadcasted_iota(jnp.int32, wide, 0)
-    kept = jnp.where(row < levels, masks[0:1, :], masks[1:2, :])
+    kept = jnp.broadcast_to(masks[...], wide)
     capacity = jnp.zeros(wide, jnp.float32)
     for index, size in enumerate(LEVELS + LEVELS[-1:] * (levels - len(LEVELS))):
-        capacity = jnp.where((row == index) | (row == index + levels), float(size), capacity)
+        capacity = jnp.where(row == index, float(size), capacity)
 
     square = (PLACES, PLACES)
     down_place, down_orbital, _, _, _ = place_facts(square, 0)
@@ -168,7 +167,6 @@
     for part in up + down + cross[0] + cross[1]:
         left = left + part
     left = jnp.sum(left, axis=1, keepdims=True)
-    left = left[:levels] + left[levels:]
     order = lax.broadcasted_iota(jnp.int32, (levels, 1), 0).astype(jnp.float32)
     level = jnp.min(jnp.where(left > 0, float(len(LEVELS) - 1), order), axis=0, keepdims=True)
     level_row = as_number(
@@ -730,11 +728,10 @@
         return product(loc, meta, sources, held, after, stages, NOB, row_blocks, col_blocks)
 
     kept = block_mask.T > 0
-    if aux_count == 4 and occ_count == 4 and shape["parts"] == 2:
+    if aux_count == 4 and occ_count == 4:
         mask = as_number(kept).reshape(1, PLACES)
-        other = lax.ppermute(mask, "parts", [(0, 1), (1, 0)])
         where = jnp.stack([aux, occ]).astype(jnp.int32)
-        table = plan(where, jnp.concatenate([mask, other]), slots)
+        table = plan(where, mask, slots)
         own = pick(factors, block_lists)
         return lax.switch(
             table[6, 0],

time: 134 us -> 126 us (0.940)
  the two profiles are of different devices: /device:TPU:8 before, /device:TPU:1 now
where the time goes in v2:
time: 126 us; the launch traced here: 125 us
  Pallas kernels  52.2 us (41%)
  waiting for transfers between devices  45.4 us (36%)
  starting transfers between devices  18 us (14%)
  local copies, waits for them, and re-layouts  6.57 us (5%)
    pallas_call x4, Pallas kernels, product(): pl.pallas_call(functools.partial(product_kernel, groups, orbitals, row_bl...  29.6 us
    ppermute x5, waiting for transfers between devices, rounds(): crossed.append(lax.ppermute(chunks[2 if turn < HOPS else 0], 'aux', across))  18.4 us
    pallas_call x5, Pallas kernels, gather(): pl.pallas_call(functools.partial(gather_kernel, turn, len(buffers), strea...  18 us
    ppermute x4, waiting for transfers between devices, rounds(): moved.append(lax.ppermute(chunks[0], 'occ', first))  17.2 us
    ppermute x6, waiting for transfers between devices, to_core(): return lax.ppermute(held, 'aux', first)  9.84 us
    ppermute x5, starting transfers between devices, rounds(): crossed.append(lax.ppermute(chunks[2 if turn < HOPS else 0], 'aux', across))  5.98 us
    ppermute x6, starting transfers between devices, to_core(): return lax.ppermute(held, 'aux', first)  4.06 us
    ppermute x4, starting transfers between devices, rounds(): moved.append(lax.ppermute(chunks[1], ('aux', 'occ'), second))  4.04 us
  transfers between devices with their start and end apart: 19, of which 11 were waited for; matrix products, arithmetic and copies ran while one was open for 0% of the time, Pallas kernels for 26%

profile of v2, /device:TPU:1, one launch (start us, length us, event | category | flops | bytes accessed | tf_op | source)
XLA Modules:
  0.0 124.6 jit_solution(15264227142271492920)
XLA Ops:
  0.9 2.4 %plan.1 = s32[8,384]{1,0:T(8,128)S(1)} custom-call(s32[2]{0:T(128)S(1)} %pad_add_fusion.where, f32[1,384]{1,0:T(1,128)S(1)} %reshape.9.masks), custom_call_target="tpu_custom_call" | custom-call | tf_op jit(solution)/shard_map/plan/pallas_call | solution.py:246
  4.5 1.8 %copy-done.20 = bf16[1,224,6144]{2,1,0:T(8,128)(2,1)S(1)} copy-done((bf16[1,224,6144]{2,1,0:T(8,128)(2,1)S(1)}, bf16[1,224,6144]{2,1,0:T(8,128)(2,1)}, u32[]{:S(2)}) %copy-start.20) | copy-done | bytes 2752536
  7.0 2.2 %pick.1 = bf16[48,112,128]{2,1,0:T(8,128)(2,1)} custom-call(s32[2,24]{1,0:T(2,128)S(1)} %copy-done.26, bf16[1,224,6144]{2,1,0:T(8,128)(2,1)S(1)} %copy-done.20), custom_call_target="tpu_custom_call" | custom-call | bytes 2752512 | tf_op jit(solution)/shard_map/pick/pallas_call | solution.py:42
  9.1 115.3 %conditional.1 = (f32[1536,1536]{1,0:T(8,128)}) conditional(s32[]{:T(128)} %bitcast.3, (s32[8,384]{1,0:T(8,128)S(1)}, bf16[48,112,128]{2,1,0:T(8,128)(2,1)}, s32[2]{0:T(128)S(1)}) %tuple.17, (s32[8,384]{1,0:T(8,128)S(1)}, bf16[48,112,128]{2,1,0:T(8,128)(2,1)}, s32[2]{0:T(128)S(1)}) %tuple.17, ...), branch_computations={%region_0.1_spmd, %region_1.2_spmd, %region_2.3_spmd, %region_3.4_... | conditional | flops 67645734912 | bytes 315010400 | solution.py:736
  9.1 2.3 %gather.25 = (bf16[18,112,128]{2,1,0:T(8,128)(2,1)S(1)}, bf16[18,112,128]{2,1,0:T(8,128)(2,1)S(1)}, bf16[18,112,128]{2,1,0:T(8,128)(2,1)S(1)}) custom-call(s32[3072]{0:T(1024)S(1)} %reshape.12.table, bf16[48,112,128]{2,1,0:T(8,128)(2,1)} %get-tuple-element.63.refs_0_.refs_1_), custom_call_target="tpu_custom_call" | custom-call | bytes 3096576 | tf_op jit(solution)/shard_map/cond/branch_1_fun/gather/pallas_call | solution.py:324
  11.4 2.2 %collective-permute-start.20 = (bf16[18,112,128]{2,1,0:T(8,128)(2,1)S(1)}, bf16[18,112,128]{2,1,0:T(8,128)(2,1)S(1)}, u32[]{:S(2)}, u32[]{:S(2)}) collective-permute-start(bf16[18,112,128]{2,1,0:T(8,128)(2,1)S(1)} %get-tuple-element.64), channel_id=1, source_target_pairs={{0,1},{1,0},{2,3},{3,2},{4,5},{5,4},{6,7},{7,6},{8,9},{9,8},{10,11... | collective-permute-start | bytes 1548296 | tf_op jit(solution)/shard_map/cond/branch_1_fun/ppermute | solution.py:713
  15.8 9.3 %collective-permute-done.20.refs_1_.refs_3_.refs_2_ = bf16[18,112,128]{2,1,0:T(8,128)(2,1)S(1)} collective-permute-done((bf16[18,112,128]{2,1,0:T(8,128)(2,1)S(1)}, bf16[18,112,128]{2,1,0:T(8,128)(2,1)S(1)}, u32[]{:S(2)}, u32[]{:S(2)}) %collective-permute-start.20) | collective-permute-done | bytes 516128 | tf_op jit(solution)/shard_map/cond/branch_1_fun/ppermute | solution.py:713
  25.1 2.9 %collective-permute-done.22.refs_5_.refs_10_.refs_15_.refs_19_ = bf16[18,112,128]{2,1,0:T(8,128)(2,1)S(1)} collective-permute-done((bf16[18,112,128]{2,1,0:T(8,128)(2,1)S(1)}, bf16[18,112,128]{2,1,0:T(8,128)(2,1)S(1)}, u32[]{:S(2)}, u32[]{:S(2)}) %collective-permute-start.22) | collective-permute-done | bytes 516128 | tf_op jit(solution)/shard_map/cond/branch_1_fun/ppermute | solution.py:716
  27.9 4.5 %gather.26 = (bf16[18,112,128]{2,1,0:T(8,128)(2,1)S(1)}, bf16[18,112,128]{2,1,0:T(8,128)(2,1)S(1)}, bf16[18,112,128]{2,1,0:T(8,128)(2,1)S(1)}, bf16[54,112,128]{2,1,0:T(8,128)(2,1)}) custom-call(s32[3072]{0:T(1024)S(1)} %reshape.12.table, bf16[48,112,128]{2,1,0:T(8,128)(2,1)} %get-tuple-element.63.refs_0_.refs_1_, ...), custom_call_target="tpu_custom_call" | custom-call | bytes 3096576 | tf_op jit(solution)/shard_map/cond/branch_1_fun/gather/pallas_call | solution.py:324
  32.4 1.8 %collective-permute-start.24 = (bf16[18,112,128]{2,1,0:T(8,128)(2,1)S(1)}, bf16[18,112,128]{2,1,0:T(8,128)(2,1)S(1)}, u32[]{:S(2)}, u32[]{:S(2)}) collective-permute-start(bf16[18,112,128]{2,1,0:T(8,128)(2,1)S(1)} %get-tuple-element.68), channel_id=1, source_target_pairs={{0,1},{1,0},{2,3},{3,2},{4,5},{5,4},{6,7},{7,6},{8,9},{9,8},{10,11... | collective-permute-start | bytes 1548296 | tf_op jit(solution)/shard_map/cond/branch_1_fun/ppermute | solution.py:713
  34.1 2.4 %collective-permute-start.25 = (bf16[18,112,128]{2,1,0:T(8,128)(2,1)S(1)}, bf16[18,112,128]{2,1,0:T(8,128)(2,1)S(1)}, u32[]{:S(2)}, u32[]{:S(2)}) collective-permute-start(bf16[18,112,128]{2,1,0:T(8,128)(2,1)S(1)} %get-tuple-element.69), channel_id=1, source_target_pairs={{0,4},{1,2},{2,1},{3,7},{4,0},{5,6},{6,5},{7,3},{8,12},{9,10},{10,... | collective-permute-start | bytes 1548296 | tf_op jit(solution)/shard_map/cond/branch_1_fun/ppermute | solution.py:714
  38.2 5.8 %collective-permute-done.24.refs_3_.refs_5_.refs_6_.refs_7_ = bf16[18,112,128]{2,1,0:T(8,128)(2,1)S(1)} collective-permute-done((bf16[18,112,128]{2,1,0:T(8,128)(2,1)S(1)}, bf16[18,112,128]{2,1,0:T(8,128)(2,1)S(1)}, u32[]{:S(2)}, u32[]{:S(2)}) %collective-permute-start.24) | collective-permute-done | bytes 516128 | tf_op jit(solution)/shard_map/cond/branch_1_fun/ppermute | solution.py:713
  44.0 5.9 %collective-permute-done.26.refs_7_.refs_12_.refs_17_.refs_21_ = bf16[18,112,128]{2,1,0:T(8,128)(2,1)S(1)} collective-permute-done((bf16[18,112,128]{2,1,0:T(8,128)(2,1)S(1)}, bf16[18,112,128]{2,1,0:T(8,128)(2,1)S(1)}, u32[]{:S(2)}, u32[]{:S(2)}) %collective-permute-start.26) | collective-permute-done | bytes 516128 | tf_op jit(solution)/shard_map/cond/branch_1_fun/ppermute | solution.py:716
  50.0 4.9 %gather.27 = (bf16[18,112,128]{2,1,0:T(8,128)(2,1)S(1)}, bf16[18,112,128]{2,1,0:T(8,128)(2,1)S(1)}, bf16[18,112,128]{2,1,0:T(8,128)(2,1)S(1)}, bf16[54,112,128]{2,1,0:T(8,128)(2,1)}) custom-call(s32[3072]{0:T(1024)S(1)} %reshape.12.table, bf16[48,112,128]{2,1,0:T(8,128)(2,1)} %get-tuple-element.63.refs_0_.refs_1_, ...), custom_call_target="tpu_custom_call" | custom-call | bytes 3096576 | tf_op jit(solution)/shard_map/cond/branch_1_fun/gather/pallas_call | solution.py:324
  60.1 4.0 %collective-permute-done.19.refs_1_.refs_2_ = bf16[48,112,128]{2,1,0:T(8,128)(2,1)} collective-permute-done((bf16[48,112,128]{2,1,0:T(8,128)(2,1)}, bf16[48,112,128]{2,1,0:T(8,128)(2,1)}, u32[]{:S(2)}, u32[]{:S(2)}) %collective-permute-start.19) | collective-permute-done | bytes 1376288 | tf_op jit(solution)/shard_map/cond/branch_1_fun/ppermute | solution.py:679
  65.2 10.9 %product.17 = (f32[1536,1536]{1,0:T(8,128)}, f32[8,128]{1,0:T(8,128)S(1)}) custom-call(s32[1152]{0:T(1024)S(1)} %reshape.16.loc, s32[2]{0:T(128)S(1)} %get-tuple-element.62.meta, bf16[48,112,128]{2,1,0:T(8,128)(2,1)} %get-tuple-element.63.refs_0_.refs_1_, bf16[48,112,128]{2,1,0:T(8,128)(2,1)} %collective-permute-done.19.refs_1_.refs_2_, ...), custom_call_target="tpu_custom_call" | custom-call | flops 16911433728 | bytes 9437184 | tf_op jit(solution)/shard_map/cond/branch_1_fun/product/pallas_call | solution.py:633
  77.3 3.5 %gather.28 = (bf16[18,112,128]{2,1,0:T(8,128)(2,1)S(1)}, bf16[18,112,128]{2,1,0:T(8,128)(2,1)S(1)}, bf16[18,112,128]{2,1,0:T(8,128)(2,1)S(1)}, bf16[54,112,128]{2,1,0:T(8,128)(2,1)S(1)}) custom-call(s32[3072]{0:T(1024)S(1)} %reshape.12.table, bf16[48,112,128]{2,1,0:T(8,128)(2,1)} %get-tuple-element.63.refs_0_.refs_1_, ...), custom_call_target="tpu_custom_call" | custom-call | bytes 3096576 | tf_op jit(solution)/shard_map/cond/branch_1_fun/gather/pallas_call | solution.py:324
  82.2 1.9 %collective-permute-start.34 = (bf16[18,112,128]{2,1,0:T(8,128)(2,1)S(1)}, bf16[18,112,128]{2,1,0:T(8,128)(2,1)S(1)}, u32[]{:S(2)}, u32[]{:S(2)}) collective-permute-start(bf16[18,112,128]{2,1,0:T(8,128)(2,1)S(1)} %get-tuple-element.81), channel_id=1, source_target_pairs={{0,8},{8,0},{4,12},{12,4},{1,9},{9,1},{5,13},{13,5},{2,10},{10,2},... | collective-permute-start | bytes 1548296 | tf_op jit(solution)/shard_map/cond/branch_1_fun/ppermute | solution.py:716
  86.2 9.6 %collective-permute-done.34.refs_11_.refs_25_ = bf16[18,112,128]{2,1,0:T(8,128)(2,1)S(1)} collective-permute-done((bf16[18,112,128]{2,1,0:T(8,128)(2,1)S(1)}, bf16[18,112,128]{2,1,0:T(8,128)(2,1)S(1)}, u32[]{:S(2)}, u32[]{:S(2)}) %collective-permute-start.34) | collective-permute-done | bytes 516128 | tf_op jit(solution)/shard_map/cond/branch_1_fun/ppermute | solution.py:716
  96.7 2.9 %gather.29 = (bf16[18,112,128]{2,1,0:T(8,128)(2,1)S(1)}, bf16[54,112,128]{2,1,0:T(8,128)(2,1)S(1)}) custom-call(s32[3072]{0:T(1024)S(1)} %reshape.12.table, bf16[48,112,128]{2,1,0:T(8,128)(2,1)} %get-tuple-element.63.refs_0_.refs_1_, bf16[18,112,128]{2,1,0:T(8,128)(2,1)S(1)} %collective-permute-done.20.refs_1_.refs_3_.refs_2_, ...), custom_call_target="tpu_custom_call" | custom-call | bytes 1032192 | tf_op jit(solution)/shard_map/cond/branch_1_fun/gather/pallas_call | solution.py:324
  101.3 3.0 %collective-permute-done.35.refs_16_.refs_18_.refs_26_ = bf16[54,112,128]{2,1,0:T(8,128)(2,1)S(1)} collective-permute-done((bf16[54,112,128]{2,1,0:T(8,128)(2,1)S(1)}, bf16[54,112,128]{2,1,0:T(8,128)(2,1)S(1)}, u32[]{:S(2)}, u32[]{:S(2)}) %collective-permute-start.35) | collective-permute-done | bytes 1548320 | tf_op jit(solution)/shard_map/cond/branch_1_fun/ppermute | solution.py:679
  104.3 15.9 %product.19 = (f32[1536,1536]{1,0:T(8,128)}, f32[8,128]{1,0:T(8,128)S(1)}) custom-call(s32[1152]{0:T(1024)S(1)} %reshape.16.loc, s32[2]{0:T(128)S(1)} %get-tuple-element.62.meta, f32[1536,1536]{1,0:T(8,128)} %get-tuple-element.79.refs_0_, bf16[48,112,128]{2,1,0:T(8,128)(2,1)} %get-tuple-element.63.refs_0_.refs_1_, ...), custom_call_target="tpu_custom_call", output_to_operand_aliasing={{0}: (2, {})} | custom-call | flops 16911433728 | bytes 9437184 | tf_op jit(solution)/shard_map/cond/branch_1_fun/product/pallas_call | solution.py:633
  120.3 1.9 %collective-permute-done.37.refs_28_ = bf16[18,112,128]{2,1,0:T(8,128)(2,1)S(1)} collective-permute-done((bf16[18,112,128]{2,1,0:T(8,128)(2,1)S(1)}, bf16[18,112,128]{2,1,0:T(8,128)(2,1)S(1)}, u32[]{:S(2)}, u32[]{:S(2)}) %collective-permute-start.37) | collective-permute-done | bytes 516128 | tf_op jit(solution)/shard_map/cond/branch_1_fun/ppermute | solution.py:679
  122.2 1.7 %product.20 = (f32[1536,1536]{1,0:T(8,128)}, f32[8,128]{1,0:T(8,128)}) custom-call(s32[1152]{0:T(1024)S(1)} %reshape.16.loc, s32[2]{0:T(128)S(1)} %get-tuple-element.62.meta, f32[1536,1536]{1,0:T(8,128)} %get-tuple-element.85.refs_0_, bf16[48,112,128]{2,1,0:T(8,128)(2,1)} %get-tuple-element.63.refs_0_.refs_1_, ...), custom_call_target="tpu_custom_call", output_to_operand_aliasing={{0}: (2, {})} | custom-call | flops 16911433728 | bytes 9437184 | tf_op jit(solution)/shard_map/cond/branch_1_fun/product/pallas_call | solution.py:633
  (47 shorter events, 19.6 us)
Async XLA Ops:
  4.5 1.8 %copy-start.20 = (bf16[1,224,6144]{2,1,0:T(8,128)(2,1)S(1)}, bf16[1,224,6144]{2,1,0:T(8,128)(2,1)}, u32[]{:S(2)}) copy-start(bf16[1,224,6144]{2,1,0:T(8,128)(2,1)} %factors.1) | copy-start | bytes 8257540
  11.4 13.7 %collective-permute-start.20 = (bf16[18,112,128]{2,1,0:T(8,128)(2,1)S(1)}, bf16[18,112,128]{2,1,0:T(8,128)(2,1)S(1)}, u32[]{:S(2)}, u32[]{:S(2)}) collective-permute-start(bf16[18,112,128]{2,1,0:T(8,128)(2,1)S(1)} %get-tuple-element.64), channel_id=1, source_target_pairs={{0,1},{1,0},{2,3},{3,2},{4,5},{5,4},{6,7},{7,6},{8,9},{9,8},{10,11... | collective-permute-start | bytes 1548296 | tf_op jit(solution)/shard_map/cond/branch_1_fun/ppermute | solution.py:713
  13.6 11.5 %collective-permute-start.21 = (bf16[18,112,128]{2,1,0:T(8,128)(2,1)S(1)}, bf16[18,112,128]{2,1,0:T(8,128)(2,1)S(1)}, u32[]{:S(2)}, u32[]{:S(2)}) collective-permute-start(bf16[18,112,128]{2,1,0:T(8,128)(2,1)S(1)} %get-tuple-element.65), channel_id=1, source_target_pairs={{0,4},{1,2},{2,1},{3,7},{4,0},{5,6},{6,5},{7,3},{8,12},{9,10},{10,... | collective-permute-start | bytes 1548296 | tf_op jit(solution)/shard_map/cond/branch_1_fun/ppermute | solution.py:714
  14.5 13.4 %collective-permute-start.22 = (bf16[18,112,128]{2,1,0:T(8,128)(2,1)S(1)}, bf16[18,112,128]{2,1,0:T(8,128)(2,1)S(1)}, u32[]{:S(2)}, u32[]{:S(2)}) collective-permute-start(bf16[18,112,128]{2,1,0:T(8,128)(2,1)S(1)} %get-tuple-element.66), channel_id=1, source_target_pairs={{0,8},{8,0},{4,12},{12,4},{1,9},{9,1},{5,13},{13,5},{2,10},{10,2},... | collective-permute-start | bytes 1548296 | tf_op jit(solution)/shard_map/cond/branch_1_fun/ppermute | solution.py:716
  32.4 11.7 %collective-permute-start.24 = (bf16[18,112,128]{2,1,0:T(8,128)(2,1)S(1)}, bf16[18,112,128]{2,1,0:T(8,128)(2,1)S(1)}, u32[]{:S(2)}, u32[]{:S(2)}) collective-permute-start(bf16[18,112,128]{2,1,0:T(8,128)(2,1)S(1)} %get-tuple-element.68), channel_id=1, source_target_pairs={{0,1},{1,0},{2,3},{3,2},{4,5},{5,4},{6,7},{7,6},{8,9},{9,8},{10,11... | collective-permute-start | bytes 1548296 | tf_op jit(solution)/shard_map/cond/branch_1_fun/ppermute | solution.py:713
  34.1 9.9 %collective-permute-start.25 = (bf16[18,112,128]{2,1,0:T(8,128)(2,1)S(1)}, bf16[18,112,128]{2,1,0:T(8,128)(2,1)S(1)}, u32[]{:S(2)}, u32[]{:S(2)}) collective-permute-start(bf16[18,112,128]{2,1,0:T(8,128)(2,1)S(1)} %get-tuple-element.69), channel_id=1, source_target_pairs={{0,4},{1,2},{2,1},{3,7},{4,0},{5,6},{6,5},{7,3},{8,12},{9,10},{10,... | collective-permute-start | bytes 1548296 | tf_op jit(solution)/shard_map/cond/branch_1_fun/ppermute | solution.py:714
  36.6 13.4 %collective-permute-start.26 = (bf16[18,112,128]{2,1,0:T(8,128)(2,1)S(1)}, bf16[18,112,128]{2,1,0:T(8,128)(2,1)S(1)}, u32[]{:S(2)}, u32[]{:S(2)}) collective-permute-start(bf16[18,112,128]{2,1,0:T(8,128)(2,1)S(1)} %get-tuple-element.70), channel_id=1, source_target_pairs={{0,8},{8,0},{4,12},{12,4},{1,9},{9,1},{5,13},{13,5},{2,10},{10,2},... | collective-permute-start | bytes 1548296 | tf_op jit(solution)/shard_map/cond/branch_1_fun/ppermute | solution.py:716
  37.9 26.2 %collective-permute-start.23 = (bf16[54,112,128]{2,1,0:T(8,128)(2,1)}, bf16[54,112,128]{2,1,0:T(8,128)(2,1)}, u32[]{:S(2)}, u32[]{:S(2)}) collective-permute-start(bf16[54,112,128]{2,1,0:T(8,128)(2,1)} %get-tuple-element.67), channel_id=1, source_target_pairs={{0,4},{4,0},{8,12},{12,8},{1,5},{5,1},{9,13},{13,9},{2,6},{6,2},{1... | collective-permute-start | bytes 4644872 | tf_op jit(solution)/shard_map/cond/branch_1_fun/ppermute | solution.py:679
  54.8 0.8 copy-start.31
  55.7 0.8 copy-start.33
  56.5 0.8 copy-start.34
  57.3 6.8 %collective-permute-start.27 = (bf16[54,112,128]{2,1,0:T(8,128)(2,1)}, bf16[54,112,128]{2,1,0:T(8,128)(2,1)}, u32[]{:S(2)}, u32[]{:S(2)}) collective-permute-start(bf16[54,112,128]{2,1,0:T(8,128)(2,1)} %get-tuple-element.71), channel_id=1, source_target_pairs={{0,4},{4,0},{8,12},{12,8},{1,5},{5,1},{9,13},{13,9},{2,6},{6,2},{1... | collective-permute-start | bytes 4644872 | tf_op jit(solution)/shard_map/cond/branch_1_fun/ppermute | solution.py:679
  58.1 6.0 %collective-permute-start.19 = (bf16[48,112,128]{2,1,0:T(8,128)(2,1)}, bf16[48,112,128]{2,1,0:T(8,128)(2,1)}, u32[]{:S(2)}, u32[]{:S(2)}) collective-permute-start(bf16[48,112,128]{2,1,0:T(8,128)(2,1)} %get-tuple-element.63.refs_0_.refs_1_), channel_id=1, source_target_pairs={{0,4},{4,0},{8,12},{12,8},{1,5},{5,1},{9,13},{13,9},{2,6},{6,2},{1... | collective-permute-start | bytes 4128776 | tf_op jit(solution)/shard_map/cond/branch_1_fun/ppermute | solution.py:679
  58.1 18.0 %collective-permute-start.29 = (bf16[18,112,128]{2,1,0:T(8,128)(2,1)}, bf16[18,112,128]{2,1,0:T(8,128)(2,1)S(1)}, u32[]{:S(2)}, u32[]{:S(2)}) collective-permute-start(bf16[18,112,128]{2,1,0:T(8,128)(2,1)} %copy-done.34), channel_id=1, source_target_pairs={{0,4},{1,2},{2,1},{3,7},{4,0},{5,6},{6,5},{7,3},{8,12},{9,10},{10,... | collective-permute-start | bytes 1548296 | tf_op jit(solution)/shard_map/cond/branch_1_fun/ppermute | solution.py:714
  58.7 17.4 %collective-permute-start.30 = (bf16[18,112,128]{2,1,0:T(8,128)(2,1)}, bf16[18,112,128]{2,1,0:T(8,128)(2,1)S(1)}, u32[]{:S(2)}, u32[]{:S(2)}) collective-permute-start(bf16[18,112,128]{2,1,0:T(8,128)(2,1)} %copy-done.33), channel_id=1, source_target_pairs={{0,8},{8,0},{4,12},{12,4},{1,9},{9,1},{5,13},{13,5},{2,10},{10,2},... | collective-permute-start | bytes 1548296 | tf_op jit(solution)/shard_map/cond/branch_1_fun/ppermute | solution.py:716
  64.1 13.2 %collective-permute-start.28 = (bf16[18,112,128]{2,1,0:T(8,128)(2,1)}, bf16[18,112,128]{2,1,0:T(8,128)(2,1)S(1)}, u32[]{:S(2)}, u32[]{:S(2)}) collective-permute-start(bf16[18,112,128]{2,1,0:T(8,128)(2,1)} %copy-done.31), channel_id=1, source_target_pairs={{0,1},{1,0},{2,3},{3,2},{4,5},{5,4},{6,7},{7,6},{8,9},{9,8},{10,11... | collective-permute-start | bytes 1548296 | tf_op jit(solution)/shard_map/cond/branch_1_fun/ppermute | solution.py:713
  64.1 1.1 copy-start.32
  80.8 4.3 %collective-permute-start.31 = (bf16[54,112,128]{2,1,0:T(8,128)(2,1)S(1)}, bf16[54,112,128]{2,1,0:T(8,128)(2,1)S(1)}, u32[]{:S(2)}, u32[]{:S(2)}) collective-permute-start(bf16[54,112,128]{2,1,0:T(8,128)(2,1)S(1)} %get-tuple-element.77), channel_id=1, source_target_pairs={{0,4},{4,0},{8,12},{12,8},{1,5},{5,1},{9,13},{13,9},{2,6},{6,2},{1... | collective-permute-start | bytes 4644872 | tf_op jit(solution)/shard_map/cond/branch_1_fun/ppermute | solution.py:679
  82.1 4.1 %collective-permute-start.33 = (bf16[18,112,128]{2,1,0:T(8,128)(2,1)S(1)}, bf16[18,112,128]{2,1,0:T(8,128)(2,1)S(1)}, u32[]{:S(2)}, u32[]{:S(2)}) collective-permute-start(bf16[18,112,128]{2,1,0:T(8,128)(2,1)S(1)} %get-tuple-element.80), channel_id=1, source_target_pairs={{0,4},{1,2},{2,1},{3,7},{4,0},{5,6},{6,5},{7,3},{8,12},{9,10},{10,... | collective-permute-start | bytes 1548296 | tf_op jit(solution)/shard_map/cond/branch_1_fun/ppermute | solution.py:714
  82.2 13.7 %collective-permute-start.34 = (bf16[18,112,128]{2,1,0:T(8,128)(2,1)S(1)}, bf16[18,112,128]{2,1,0:T(8,128)(2,1)S(1)}, u32[]{:S(2)}, u32[]{:S(2)}) collective-permute-start(bf16[18,112,128]{2,1,0:T(8,128)(2,1)S(1)} %get-tuple-element.81), channel_id=1, source_target_pairs={{0,8},{8,0},{4,12},{12,4},{1,9},{9,1},{5,13},{13,5},{2,10},{10,2},... | collective-permute-start | bytes 1548296 | tf_op jit(solution)/shard_map/cond/branch_1_fun/ppermute | solution.py:716
  84.1 12.6 %collective-permute-start.32 = (bf16[18,112,128]{2,1,0:T(8,128)(2,1)S(1)}, bf16[18,112,128]{2,1,0:T(8,128)(2,1)S(1)}, u32[]{:S(2)}, u32[]{:S(2)}) collective-permute-start(bf16[18,112,128]{2,1,0:T(8,128)(2,1)S(1)} %get-tuple-element.78.refs_21_), channel_id=1, source_target_pairs={{0,1},{1,0},{2,3},{3,2},{4,5},{5,4},{6,7},{7,6},{8,9},{9,8},{10,11... | collective-permute-start | bytes 1548296 | tf_op jit(solution)/shard_map/cond/branch_1_fun/ppermute | solution.py:713
  99.6 4.7 %collective-permute-start.35 = (bf16[54,112,128]{2,1,0:T(8,128)(2,1)S(1)}, bf16[54,112,128]{2,1,0:T(8,128)(2,1)S(1)}, u32[]{:S(2)}, u32[]{:S(2)}) collective-permute-start(bf16[54,112,128]{2,1,0:T(8,128)(2,1)S(1)} %get-tuple-element.83), channel_id=1, source_target_pairs={{0,4},{4,0},{8,12},{12,8},{1,5},{5,1},{9,13},{13,9},{2,6},{6,2},{1... | collective-permute-start | bytes 4644872 | tf_op jit(solution)/shard_map/cond/branch_1_fun/ppermute | solution.py:679
  101.3 18.9 %collective-permute-start.36 = (bf16[18,112,128]{2,1,0:T(8,128)(2,1)S(1)}, bf16[18,112,128]{2,1,0:T(8,128)(2,1)S(1)}, u32[]{:S(2)}, u32[]{:S(2)}) collective-permute-start(bf16[18,112,128]{2,1,0:T(8,128)(2,1)S(1)} %get-tuple-element.84.refs_27_), channel_id=1, source_target_pairs={{0,8},{8,0},{4,12},{12,4},{1,9},{9,1},{5,13},{13,5},{2,10},{10,2},... | collective-permute-start | bytes 1548296 | tf_op jit(solution)/shard_map/cond/branch_1_fun/ppermute | solution.py:716
  120.2 2.0 %collective-permute-start.37 = (bf16[18,112,128]{2,1,0:T(8,128)(2,1)S(1)}, bf16[18,112,128]{2,1,0:T(8,128)(2,1)S(1)}, u32[]{:S(2)}, u32[]{:S(2)}) collective-permute-start(bf16[18,112,128]{2,1,0:T(8,128)(2,1)S(1)} %relay.4), channel_id=1, source_target_pairs={{0,4},{4,0},{8,12},{12,8},{1,5},{5,1},{9,13},{13,9},{2,6},{6,2},{1... | collective-permute-start | bytes 1548296 | tf_op jit(solution)/shard_map/cond/branch_1_fun/ppermute | solution.py:679
  (1 other events, 0.7 us)
